TPU v7x, 512 devices: a whole 4x8x8 slice. The times are simulated.
512 devices in a mesh: seq: 16 (over z, core), grp: 32 (over x, y).
Axes of the slice: x: 4, y: 8, z: 8, core: 2. Of those that a mesh axis runs over, the one named last changes fastest.
Arguments:
- post_gate: bfloat16 [2048, 8192], P('seq', 'grp'), may hold values from -6 to 6
- pre_gate: bfloat16 [2048, 8192], P('seq', 'grp'), may hold values from -6 to 6
- values_in: bfloat16 [2048, 8192], P('seq', 'grp'), may hold values from -6 to 6
- filters: bfloat16 [512, 2048], P('grp'), may hold values from -1 to 1
- grad_out: bfloat16 [2048, 8192], P('seq', 'grp'), may hold values from -6 to 6
Outputs:
- output: bfloat16 [2048, 8192], P('seq', 'grp')
- grad_post: bfloat16 [2048, 8192], P('seq', 'grp')
- grad_pre: bfloat16 [2048, 8192], P('seq', 'grp')
- grad_values: bfloat16 [2048, 8192], P('seq', 'grp')
- grad_filters: float32 [512, 2048], P('grp', 'seq')
All inputs are finite; a program needn't handle non-finite values.
Results may differ from a plain program's by a relative error of at most 0.0049.
Values may be sent and summed in bfloat16 or wider, within the bound.
No kernel may reach another device: no remote copies, remote signals or barrier semaphores. Data moves between devices by JAX's collectives and lax.ppermute only.
A program may use at most 64 MiB of HBM per device.

v0:
```python
import math

import jax
import jax.numpy as jnp
from jax import lax
from jax.sharding import PartitionSpec as P

GROUP = 16


def toeplitz(padded_row, distance, width):
    length = padded_row.shape[0] // 2
    begin_at = length + distance * width - width + 1
    segment = lax.dynamic_slice_in_dim(padded_row, begin_at, 2 * width - 1, 0)
    extended = jnp.concatenate([segment, jnp.zeros((1,), segment.dtype)])
    flat = jnp.tile(extended, width + 1)[: width * (2 * width + 1)]
    return flat.reshape(width, 2 * width + 1)[:, :width][:, ::-1]


def diagonal_sums(product):
    width = product.shape[0]
    flipped = product[:, ::-1]
    widened = jnp.concatenate([flipped, jnp.zeros((width, width), product.dtype)], axis=1)
    skewed = widened.reshape(-1)[: width * (2 * width - 1)].reshape(width, 2 * width - 1)
    return jnp.sum(skewed, axis=0)


def lags_from_distances(dist, width, length):
    n_blocks = dist.shape[0]
    n_filters = dist.shape[1]
    upper = dist[:, :, width - 1 :]
    lower = jnp.concatenate(
        [jnp.zeros((n_blocks, n_filters, 1), jnp.float32), dist[:, :, : width - 1]], axis=2
    )
    blocks_lag = upper + jnp.concatenate(
        [lower[1:], jnp.zeros((1, n_filters, width), jnp.float32)], axis=0
    )
    return blocks_lag.transpose(1, 0, 2).reshape(n_filters, length)


def on_device(post_gate, pre_gate, values_in, filters, grad_out):
    tok_rows, channels = post_gate.shape
    groups_dev, length = filters.shape
    shards = lax.axis_size("seq")
    own_idx = lax.axis_index("seq")
    mixed_in = (pre_gate.astype(jnp.float32) * values_in.astype(jnp.float32)).astype(jnp.bfloat16)
    grad_mix = (grad_out.astype(jnp.float32) * post_gate.astype(jnp.float32)).astype(jnp.bfloat16)
    padded = jnp.concatenate([jnp.zeros((groups_dev, length), jnp.bfloat16), filters], axis=1)

    def by_group(block):
        return block.reshape(tok_rows, groups_dev, GROUP).transpose(1, 0, 2)

    gm_groups = by_group(grad_mix)
    zero_filt = jnp.zeros((groups_dev, tok_rows, GROUP), jnp.float32)
    zero_dist = jnp.zeros((shards, groups_dev, 2 * tok_rows - 1), jnp.float32)
    incoming = lax.all_gather(mixed_in[None], "seq", axis=0, tiled=True)
    n_in = incoming.shape[0]

    def forward_one_shard(current, member):
        block, offset = member
        distance = own_idx - offset

        def forward_work(state):
            filt, dist = state

            def forward_one_group(item):
                hrow, source, grads = item
                kern = toeplitz(hrow, distance, tok_rows)
                part = jnp.dot(kern, source, preferred_element_type=jnp.float32)
                pair = jnp.einsum("ag,bg->ab", grads, source, preferred_element_type=jnp.float32)
                return (part, diagonal_sums(pair))

            parts, diags = lax.map(forward_one_group, (padded, by_group(block), gm_groups))
            before = lax.dynamic_index_in_dim(dist, distance, 0, keepdims=False)
            return (
                filt + parts,
                lax.dynamic_update_index_in_dim(dist, before + diags, distance, 0),
            )

        return (lax.cond(distance >= 0, forward_work, lambda state: state, current), None)

    result, _ = lax.scan(
        forward_one_shard, (zero_filt, zero_dist), (incoming, jnp.arange(n_in, dtype=jnp.int32))
    )
    filt, dist = result
    incoming = lax.all_gather(grad_mix[None], "seq", axis=0, tiled=True)
    n_in = incoming.shape[0]

    def backward_one_shard(current, member):
        block, offset = member
        distance = offset - own_idx

        def backward_work(back):

            def backward_one_group(item):
                hrow, grads = item
                kern = toeplitz(hrow, distance, tok_rows)
                return jnp.einsum("ab,ag->bg", kern, grads, preferred_element_type=jnp.float32)

            return back + lax.map(backward_one_group, (padded, by_group(block)))

        return (lax.cond(distance >= 0, backward_work, lambda back: back, current), None)

    result, _ = lax.scan(
        backward_one_shard, zero_filt, (incoming, jnp.arange(n_in, dtype=jnp.int32))
    )
    back = result
    filtered = filt.transpose(1, 0, 2).reshape(tok_rows, channels)
    grad_mixed = back.transpose(1, 0, 2).reshape(tok_rows, channels)
    lag_full = lags_from_distances(dist, tok_rows, length)
    filter_grad = lax.psum_scatter(lag_full, "seq", scatter_dimension=1, tiled=True)
    grad_scale = 1.0 / math.sqrt(GROUP * length)
    output = (post_gate.astype(jnp.float32) * filtered).astype(jnp.bfloat16)
    grad_post = (grad_out.astype(jnp.float32) * filtered).astype(jnp.bfloat16)
    grad_pre = (grad_mixed * values_in.astype(jnp.float32)).astype(jnp.bfloat16)
    grad_values = (grad_mixed * pre_gate.astype(jnp.float32)).astype(jnp.bfloat16)
    return (output, grad_post, grad_pre, grad_values, filter_grad * grad_scale)


def solution(mesh):
    return jax.shard_map(
        on_device,
        mesh=mesh,
        in_specs=(
            P("seq", "grp"),
            P("seq", "grp"),
            P("seq", "grp"),
            P("grp", None),
            P("seq", "grp"),
        ),
        out_specs=(
            P("seq", "grp"),
            P("seq", "grp"),
            P("seq", "grp"),
            P("seq", "grp"),
            P("grp", "seq"),
        ),
        check_vma=False,
    )
```

profile of v0, /device:TPU:1, one launch (start us, length us, event | category | flops | bytes accessed | tf_op | source)
XLA Modules:
  0.0 974.1 jit_solution(10116255169346689235)
XLA Ops:
  7.2 0.9 copy.27
  11.5 46.0 %all-gather.7.cloned.1.call-done = bf16[2048,256]{0,1:T(8,128)(2,1)} async-done(((bf16[128,256]{0,1:T(8,128)(2,1)}), bf16[2048,256]{0,1:T(8,128)(2,1)}) %all-gather.7.cloned.1.call-update) | async-done | bytes 1048592 | tf_op jit(solution)/shard_map/all_gather | solution.py:86
  57.5 1.5 copy_bitcast_fusion
  59.0 202.1 %while.59 = (s32[]{:T(128)}, f32[16,128,16]{1,2,0:T(8,128)S(1)}, s32[16]{0:T(128)S(1)}, s32[]{:T(128)}, bf16[16,128,256]{1,2,0:T(8,128)(2,1)S(1)}, /*index=5*/bf16[16,4096]{1,0:T(8,128)(2,1)S(1)}, s32[]{:T(128)}, s32[]{:T(128)}) while((s32[]{:T(128)}, f32[16,128,16]{1,2,0:T(8,128)S(1)}, s32[16]{0:T(128)S(1)}, s32[]{:T(128)}, ...), condition=%wide.region_12.13_spmd, body=%wide.region_7.12_spmd.sunk | while | flops 558094 | bytes 1034170 | solution.py:104
  61.6 12.1 %conditional.5 = (f32[16,128,16]{1,2,0:T(8,128)S(1)}) conditional(s32[]{:T(128)} %convert_element_type.83, f32[16,128,16]{1,2,0:T(8,128)S(1)} %get-tuple-element.805, (bf16[16,128,256]{1,2,0:T(8,128)(2,1)S(1)}, s32[]{:T(128)}, s32[]{:T(128)}, bf16[16,4096]{1,0:T(8,128)(2,1)S(1)}, f32[16,128,16]{1,2,0:T(8,128)S(1)}) %tuple.118), branch_computations={%region_8.8_spmd, %region_9.11_spmd} | conditional | flops 558089 | bytes 1034007 | solution.py:102
  61.6 12.0 %while.57 = (s32[]{:T(128)}, f32[16,128,16]{1,2,0:T(8,128)S(1)}, bf16[16,4096]{1,0:T(8,128)(2,1)S(1)}, s32[]{:T(128)}, bf16[16,128,16]{1,2,0:T(8,128)(2,1)S(1)},...) while((s32[]{:T(128)}, f32[16,128,16]{1,2,0:T(8,128)S(1)}, bf16[16,4096]{1,0:T(8,128)(2,1)S(1)}, ...), condition=%wide.region_11.10_spmd, body=%wide.region_10.9_spmd.sunk | while | flops 525315 | bytes 509553 | solution.py:100
  74.9 12.1 %conditional.5 = (f32[16,128,16]{1,2,0:T(8,128)S(1)}) conditional(s32[]{:T(128)} %convert_element_type.83, f32[16,128,16]{1,2,0:T(8,128)S(1)} %get-tuple-element.805, (bf16[16,128,256]{1,2,0:T(8,128)(2,1)S(1)}, s32[]{:T(128)}, s32[]{:T(128)}, bf16[16,4096]{1,0:T(8,128)(2,1)S(1)}, f32[16,128,16]{1,2,0:T(8,128)S(1)}) %tuple.118), branch_computations={%region_8.8_spmd, %region_9.11_spmd} | conditional | flops 558089 | bytes 1034007 | solution.py:102
  75.0 12.0 %while.57 = (s32[]{:T(128)}, f32[16,128,16]{1,2,0:T(8,128)S(1)}, bf16[16,4096]{1,0:T(8,128)(2,1)S(1)}, s32[]{:T(128)}, bf16[16,128,16]{1,2,0:T(8,128)(2,1)S(1)},...) while((s32[]{:T(128)}, f32[16,128,16]{1,2,0:T(8,128)S(1)}, bf16[16,4096]{1,0:T(8,128)(2,1)S(1)}, ...), condition=%wide.region_11.10_spmd, body=%wide.region_10.9_spmd.sunk | while | flops 525315 | bytes 509553 | solution.py:100
  88.3 12.1 %conditional.5 = (f32[16,128,16]{1,2,0:T(8,128)S(1)}) conditional(s32[]{:T(128)} %convert_element_type.83, f32[16,128,16]{1,2,0:T(8,128)S(1)} %get-tuple-element.805, (bf16[16,128,256]{1,2,0:T(8,128)(2,1)S(1)}, s32[]{:T(128)}, s32[]{:T(128)}, bf16[16,4096]{1,0:T(8,128)(2,1)S(1)}, f32[16,128,16]{1,2,0:T(8,128)S(1)}) %tuple.118), branch_computations={%region_8.8_spmd, %region_9.11_spmd} | conditional | flops 558089 | bytes 1034007 | solution.py:102
  88.4 12.0 %while.57 = (s32[]{:T(128)}, f32[16,128,16]{1,2,0:T(8,128)S(1)}, bf16[16,4096]{1,0:T(8,128)(2,1)S(1)}, s32[]{:T(128)}, bf16[16,128,16]{1,2,0:T(8,128)(2,1)S(1)},...) while((s32[]{:T(128)}, f32[16,128,16]{1,2,0:T(8,128)S(1)}, bf16[16,4096]{1,0:T(8,128)(2,1)S(1)}, ...), condition=%wide.region_11.10_spmd, body=%wide.region_10.9_spmd.sunk | while | flops 525315 | bytes 509553 | solution.py:100
  101.7 12.1 %conditional.5 = (f32[16,128,16]{1,2,0:T(8,128)S(1)}) conditional(s32[]{:T(128)} %convert_element_type.83, f32[16,128,16]{1,2,0:T(8,128)S(1)} %get-tuple-element.805, (bf16[16,128,256]{1,2,0:T(8,128)(2,1)S(1)}, s32[]{:T(128)}, s32[]{:T(128)}, bf16[16,4096]{1,0:T(8,128)(2,1)S(1)}, f32[16,128,16]{1,2,0:T(8,128)S(1)}) %tuple.118), branch_computations={%region_8.8_spmd, %region_9.11_spmd} | conditional | flops 558089 | bytes 1034007 | solution.py:102
  101.8 12.0 %while.57 = (s32[]{:T(128)}, f32[16,128,16]{1,2,0:T(8,128)S(1)}, bf16[16,4096]{1,0:T(8,128)(2,1)S(1)}, s32[]{:T(128)}, bf16[16,128,16]{1,2,0:T(8,128)(2,1)S(1)},...) while((s32[]{:T(128)}, f32[16,128,16]{1,2,0:T(8,128)S(1)}, bf16[16,4096]{1,0:T(8,128)(2,1)S(1)}, ...), condition=%wide.region_11.10_spmd, body=%wide.region_10.9_spmd.sunk | while | flops 525315 | bytes 509553 | solution.py:100
  115.1 12.1 %conditional.5 = (f32[16,128,16]{1,2,0:T(8,128)S(1)}) conditional(s32[]{:T(128)} %convert_element_type.83, f32[16,128,16]{1,2,0:T(8,128)S(1)} %get-tuple-element.805, (bf16[16,128,256]{1,2,0:T(8,128)(2,1)S(1)}, s32[]{:T(128)}, s32[]{:T(128)}, bf16[16,4096]{1,0:T(8,128)(2,1)S(1)}, f32[16,128,16]{1,2,0:T(8,128)S(1)}) %tuple.118), branch_computations={%region_8.8_spmd, %region_9.11_spmd} | conditional | flops 558089 | bytes 1034007 | solution.py:102
  115.2 12.0 %while.57 = (s32[]{:T(128)}, f32[16,128,16]{1,2,0:T(8,128)S(1)}, bf16[16,4096]{1,0:T(8,128)(2,1)S(1)}, s32[]{:T(128)}, bf16[16,128,16]{1,2,0:T(8,128)(2,1)S(1)},...) while((s32[]{:T(128)}, f32[16,128,16]{1,2,0:T(8,128)S(1)}, bf16[16,4096]{1,0:T(8,128)(2,1)S(1)}, ...), condition=%wide.region_11.10_spmd, body=%wide.region_10.9_spmd.sunk | while | flops 525315 | bytes 509553 | solution.py:100
  128.5 12.1 %conditional.5 = (f32[16,128,16]{1,2,0:T(8,128)S(1)}) conditional(s32[]{:T(128)} %convert_element_type.83, f32[16,128,16]{1,2,0:T(8,128)S(1)} %get-tuple-element.805, (bf16[16,128,256]{1,2,0:T(8,128)(2,1)S(1)}, s32[]{:T(128)}, s32[]{:T(128)}, bf16[16,4096]{1,0:T(8,128)(2,1)S(1)}, f32[16,128,16]{1,2,0:T(8,128)S(1)}) %tuple.118), branch_computations={%region_8.8_spmd, %region_9.11_spmd} | conditional | flops 558089 | bytes 1034007 | solution.py:102
  128.5 12.0 %while.57 = (s32[]{:T(128)}, f32[16,128,16]{1,2,0:T(8,128)S(1)}, bf16[16,4096]{1,0:T(8,128)(2,1)S(1)}, s32[]{:T(128)}, bf16[16,128,16]{1,2,0:T(8,128)(2,1)S(1)},...) while((s32[]{:T(128)}, f32[16,128,16]{1,2,0:T(8,128)S(1)}, bf16[16,4096]{1,0:T(8,128)(2,1)S(1)}, ...), condition=%wide.region_11.10_spmd, body=%wide.region_10.9_spmd.sunk | while | flops 525315 | bytes 509553 | solution.py:100
  141.9 12.1 %conditional.5 = (f32[16,128,16]{1,2,0:T(8,128)S(1)}) conditional(s32[]{:T(128)} %convert_element_type.83, f32[16,128,16]{1,2,0:T(8,128)S(1)} %get-tuple-element.805, (bf16[16,128,256]{1,2,0:T(8,128)(2,1)S(1)}, s32[]{:T(128)}, s32[]{:T(128)}, bf16[16,4096]{1,0:T(8,128)(2,1)S(1)}, f32[16,128,16]{1,2,0:T(8,128)S(1)}) %tuple.118), branch_computations={%region_8.8_spmd, %region_9.11_spmd} | conditional | flops 558089 | bytes 1034007 | solution.py:102
  141.9 12.0 %while.57 = (s32[]{:T(128)}, f32[16,128,16]{1,2,0:T(8,128)S(1)}, bf16[16,4096]{1,0:T(8,128)(2,1)S(1)}, s32[]{:T(128)}, bf16[16,128,16]{1,2,0:T(8,128)(2,1)S(1)},...) while((s32[]{:T(128)}, f32[16,128,16]{1,2,0:T(8,128)S(1)}, bf16[16,4096]{1,0:T(8,128)(2,1)S(1)}, ...), condition=%wide.region_11.10_spmd, body=%wide.region_10.9_spmd.sunk | while | flops 525315 | bytes 509553 | solution.py:100
  155.3 12.1 %conditional.5 = (f32[16,128,16]{1,2,0:T(8,128)S(1)}) conditional(s32[]{:T(128)} %convert_element_type.83, f32[16,128,16]{1,2,0:T(8,128)S(1)} %get-tuple-element.805, (bf16[16,128,256]{1,2,0:T(8,128)(2,1)S(1)}, s32[]{:T(128)}, s32[]{:T(128)}, bf16[16,4096]{1,0:T(8,128)(2,1)S(1)}, f32[16,128,16]{1,2,0:T(8,128)S(1)}) %tuple.118), branch_computations={%region_8.8_spmd, %region_9.11_spmd} | conditional | flops 558089 | bytes 1034007 | solution.py:102
  155.3 12.0 %while.57 = (s32[]{:T(128)}, f32[16,128,16]{1,2,0:T(8,128)S(1)}, bf16[16,4096]{1,0:T(8,128)(2,1)S(1)}, s32[]{:T(128)}, bf16[16,128,16]{1,2,0:T(8,128)(2,1)S(1)},...) while((s32[]{:T(128)}, f32[16,128,16]{1,2,0:T(8,128)S(1)}, bf16[16,4096]{1,0:T(8,128)(2,1)S(1)}, ...), condition=%wide.region_11.10_spmd, body=%wide.region_10.9_spmd.sunk | while | flops 525315 | bytes 509553 | solution.py:100
  168.6 12.1 %conditional.5 = (f32[16,128,16]{1,2,0:T(8,128)S(1)}) conditional(s32[]{:T(128)} %convert_element_type.83, f32[16,128,16]{1,2,0:T(8,128)S(1)} %get-tuple-element.805, (bf16[16,128,256]{1,2,0:T(8,128)(2,1)S(1)}, s32[]{:T(128)}, s32[]{:T(128)}, bf16[16,4096]{1,0:T(8,128)(2,1)S(1)}, f32[16,128,16]{1,2,0:T(8,128)S(1)}) %tuple.118), branch_computations={%region_8.8_spmd, %region_9.11_spmd} | conditional | flops 558089 | bytes 1034007 | solution.py:102
  168.7 12.0 %while.57 = (s32[]{:T(128)}, f32[16,128,16]{1,2,0:T(8,128)S(1)}, bf16[16,4096]{1,0:T(8,128)(2,1)S(1)}, s32[]{:T(128)}, bf16[16,128,16]{1,2,0:T(8,128)(2,1)S(1)},...) while((s32[]{:T(128)}, f32[16,128,16]{1,2,0:T(8,128)S(1)}, bf16[16,4096]{1,0:T(8,128)(2,1)S(1)}, ...), condition=%wide.region_11.10_spmd, body=%wide.region_10.9_spmd.sunk | while | flops 525315 | bytes 509553 | solution.py:100
  182.0 12.1 %conditional.5 = (f32[16,128,16]{1,2,0:T(8,128)S(1)}) conditional(s32[]{:T(128)} %convert_element_type.83, f32[16,128,16]{1,2,0:T(8,128)S(1)} %get-tuple-element.805, (bf16[16,128,256]{1,2,0:T(8,128)(2,1)S(1)}, s32[]{:T(128)}, s32[]{:T(128)}, bf16[16,4096]{1,0:T(8,128)(2,1)S(1)}, f32[16,128,16]{1,2,0:T(8,128)S(1)}) %tuple.118), branch_computations={%region_8.8_spmd, %region_9.11_spmd} | conditional | flops 558089 | bytes 1034007 | solution.py:102
  182.1 12.0 %while.57 = (s32[]{:T(128)}, f32[16,128,16]{1,2,0:T(8,128)S(1)}, bf16[16,4096]{1,0:T(8,128)(2,1)S(1)}, s32[]{:T(128)}, bf16[16,128,16]{1,2,0:T(8,128)(2,1)S(1)},...) while((s32[]{:T(128)}, f32[16,128,16]{1,2,0:T(8,128)S(1)}, bf16[16,4096]{1,0:T(8,128)(2,1)S(1)}, ...), condition=%wide.region_11.10_spmd, body=%wide.region_10.9_spmd.sunk | while | flops 525315 | bytes 509553 | solution.py:100
  195.4 12.1 %conditional.5 = (f32[16,128,16]{1,2,0:T(8,128)S(1)}) conditional(s32[]{:T(128)} %convert_element_type.83, f32[16,128,16]{1,2,0:T(8,128)S(1)} %get-tuple-element.805, (bf16[16,128,256]{1,2,0:T(8,128)(2,1)S(1)}, s32[]{:T(128)}, s32[]{:T(128)}, bf16[16,4096]{1,0:T(8,128)(2,1)S(1)}, f32[16,128,16]{1,2,0:T(8,128)S(1)}) %tuple.118), branch_computations={%region_8.8_spmd, %region_9.11_spmd} | conditional | flops 558089 | bytes 1034007 | solution.py:102
  195.5 12.0 %while.57 = (s32[]{:T(128)}, f32[16,128,16]{1,2,0:T(8,128)S(1)}, bf16[16,4096]{1,0:T(8,128)(2,1)S(1)}, s32[]{:T(128)}, bf16[16,128,16]{1,2,0:T(8,128)(2,1)S(1)},...) while((s32[]{:T(128)}, f32[16,128,16]{1,2,0:T(8,128)S(1)}, bf16[16,4096]{1,0:T(8,128)(2,1)S(1)}, ...), condition=%wide.region_11.10_spmd, body=%wide.region_10.9_spmd.sunk | while | flops 525315 | bytes 509553 | solution.py:100
  208.8 12.1 %conditional.5 = (f32[16,128,16]{1,2,0:T(8,128)S(1)}) conditional(s32[]{:T(128)} %convert_element_type.83, f32[16,128,16]{1,2,0:T(8,128)S(1)} %get-tuple-element.805, (bf16[16,128,256]{1,2,0:T(8,128)(2,1)S(1)}, s32[]{:T(128)}, s32[]{:T(128)}, bf16[16,4096]{1,0:T(8,128)(2,1)S(1)}, f32[16,128,16]{1,2,0:T(8,128)S(1)}) %tuple.118), branch_computations={%region_8.8_spmd, %region_9.11_spmd} | conditional | flops 558089 | bytes 1034007 | solution.py:102
  208.9 12.0 %while.57 = (s32[]{:T(128)}, f32[16,128,16]{1,2,0:T(8,128)S(1)}, bf16[16,4096]{1,0:T(8,128)(2,1)S(1)}, s32[]{:T(128)}, bf16[16,128,16]{1,2,0:T(8,128)(2,1)S(1)},...) while((s32[]{:T(128)}, f32[16,128,16]{1,2,0:T(8,128)S(1)}, bf16[16,4096]{1,0:T(8,128)(2,1)S(1)}, ...), condition=%wide.region_11.10_spmd, body=%wide.region_10.9_spmd.sunk | while | flops 525315 | bytes 509553 | solution.py:100
  222.2 12.1 %conditional.5 = (f32[16,128,16]{1,2,0:T(8,128)S(1)}) conditional(s32[]{:T(128)} %convert_element_type.83, f32[16,128,16]{1,2,0:T(8,128)S(1)} %get-tuple-element.805, (bf16[16,128,256]{1,2,0:T(8,128)(2,1)S(1)}, s32[]{:T(128)}, s32[]{:T(128)}, bf16[16,4096]{1,0:T(8,128)(2,1)S(1)}, f32[16,128,16]{1,2,0:T(8,128)S(1)}) %tuple.118), branch_computations={%region_8.8_spmd, %region_9.11_spmd} | conditional | flops 558089 | bytes 1034007 | solution.py:102
  222.2 12.0 %while.57 = (s32[]{:T(128)}, f32[16,128,16]{1,2,0:T(8,128)S(1)}, bf16[16,4096]{1,0:T(8,128)(2,1)S(1)}, s32[]{:T(128)}, bf16[16,128,16]{1,2,0:T(8,128)(2,1)S(1)},...) while((s32[]{:T(128)}, f32[16,128,16]{1,2,0:T(8,128)S(1)}, bf16[16,4096]{1,0:T(8,128)(2,1)S(1)}, ...), condition=%wide.region_11.10_spmd, body=%wide.region_10.9_spmd.sunk | while | flops 525315 | bytes 509553 | solution.py:100
  235.6 12.1 %conditional.5 = (f32[16,128,16]{1,2,0:T(8,128)S(1)}) conditional(s32[]{:T(128)} %convert_element_type.83, f32[16,128,16]{1,2,0:T(8,128)S(1)} %get-tuple-element.805, (bf16[16,128,256]{1,2,0:T(8,128)(2,1)S(1)}, s32[]{:T(128)}, s32[]{:T(128)}, bf16[16,4096]{1,0:T(8,128)(2,1)S(1)}, f32[16,128,16]{1,2,0:T(8,128)S(1)}) %tuple.118), branch_computations={%region_8.8_spmd, %region_9.11_spmd} | conditional | flops 558089 | bytes 1034007 | solution.py:102
  235.6 12.0 %while.57 = (s32[]{:T(128)}, f32[16,128,16]{1,2,0:T(8,128)S(1)}, bf16[16,4096]{1,0:T(8,128)(2,1)S(1)}, s32[]{:T(128)}, bf16[16,128,16]{1,2,0:T(8,128)(2,1)S(1)},...) while((s32[]{:T(128)}, f32[16,128,16]{1,2,0:T(8,128)S(1)}, bf16[16,4096]{1,0:T(8,128)(2,1)S(1)}, ...), condition=%wide.region_11.10_spmd, body=%wide.region_10.9_spmd.sunk | while | flops 525315 | bytes 509553 | solution.py:100
  249.0 12.1 %conditional.5 = (f32[16,128,16]{1,2,0:T(8,128)S(1)}) conditional(s32[]{:T(128)} %convert_element_type.83, f32[16,128,16]{1,2,0:T(8,128)S(1)} %get-tuple-element.805, (bf16[16,128,256]{1,2,0:T(8,128)(2,1)S(1)}, s32[]{:T(128)}, s32[]{:T(128)}, bf16[16,4096]{1,0:T(8,128)(2,1)S(1)}, f32[16,128,16]{1,2,0:T(8,128)S(1)}) %tuple.118), branch_computations={%region_8.8_spmd, %region_9.11_spmd} | conditional | flops 558089 | bytes 1034007 | solution.py:102
  249.0 12.0 %while.57 = (s32[]{:T(128)}, f32[16,128,16]{1,2,0:T(8,128)S(1)}, bf16[16,4096]{1,0:T(8,128)(2,1)S(1)}, s32[]{:T(128)}, bf16[16,128,16]{1,2,0:T(8,128)(2,1)S(1)},...) while((s32[]{:T(128)}, f32[16,128,16]{1,2,0:T(8,128)S(1)}, bf16[16,4096]{1,0:T(8,128)(2,1)S(1)}, ...), condition=%wide.region_11.10_spmd, body=%wide.region_10.9_spmd.sunk | while | flops 525315 | bytes 509553 | solution.py:100
  261.8 48.9 %all-gather.5.cloned.1.call-done = bf16[2048,256]{0,1:T(8,128)(2,1)} async-done(((bf16[128,256]{0,1:T(8,128)(2,1)}), bf16[2048,256]{0,1:T(8,128)(2,1)}) %all-gather.5.cloned.1.call-update) | async-done | bytes 1048592 | tf_op jit(solution)/shard_map/all_gather | solution.py:56
  310.7 1.5 copy_bitcast_fusion.1
  312.3 92.8 %while.58 = (s32[]{:T(128)}, f32[16,128,16]{1,2,0:T(8,128)S(1)}, f32[16,16,255]{2,1,0:T(8,128)S(1)}, s32[16]{0:T(128)S(1)}, s32[]{:T(128)}, /*index=5*/bf16[16,1...) while((s32[]{:T(128)}, f32[16,128,16]{1,2,0:T(8,128)S(1)}, ...), condition=%wide.region_6.7_spmd, body=%wide.region_0.6_spmd.sunk | while | flops 1118850 | bytes 2175440 | solution.py:82
  313.5 36.2 %conditional.4 = ((f32[16,128,16]{1,2,0:T(8,128)S(1)}, f32[16,16,255]{2,1,0:T(8,128)S(1)})) conditional(s32[]{:T(128)} %convert_element_type.82, (f32[16,128,16]{1,2,0:T(8,128)S(1)}, f32[16,16,255]{2,1,0:T(8,128)S(1)}) %tuple.115, (bf16[16,128,256]{1,2,0:T(8,128)(2,1)S(1)}, s32[]{:T(128)}, s32[]{:T(128)}, bf16[16,4096]{1,0:T(8,128)(2,1)S(1)}, ...), branch_computations={%region_1.1_spmd, %region_2.5_spmd} | conditional | flops 1118845 | bytes 2175229 | solution.py:80
  313.6 36.0 %while.56 = (s32[]{:T(128)}, f32[16,128,16]{1,2,0:T(8,128)S(1)}, f32[16,255]{1,0:T(8,128)S(1)}, bf16[16,4096]{1,0:T(8,128)(2,1)S(1)}, s32[]{:T(128)}, /*index=5*...) while((s32[]{:T(128)}, f32[16,128,16]{1,2,0:T(8,128)S(1)}, ...), condition=%wide.region_5.4_spmd, body=%wide.region_3.3_spmd.sunk | while | flops 1081988 | bytes 1568901 | solution.py:73
  325.6 0.9 fusion.41
  327.9 0.9 fusion.41
  330.1 0.9 fusion.41
  332.4 0.9 fusion.41
  345.9 0.9 fusion.41
  351.0 36.2 %conditional.4 = ((f32[16,128,16]{1,2,0:T(8,128)S(1)}, f32[16,16,255]{2,1,0:T(8,128)S(1)})) conditional(s32[]{:T(128)} %convert_element_type.82, (f32[16,128,16]{1,2,0:T(8,128)S(1)}, f32[16,16,255]{2,1,0:T(8,128)S(1)}) %tuple.115, (bf16[16,128,256]{1,2,0:T(8,128)(2,1)S(1)}, s32[]{:T(128)}, s32[]{:T(128)}, bf16[16,4096]{1,0:T(8,128)(2,1)S(1)}, ...), branch_computations={%region_1.1_spmd, %region_2.5_spmd} | conditional | flops 1118845 | bytes 2175229 | solution.py:80
  351.0 36.0 %while.56 = (s32[]{:T(128)}, f32[16,128,16]{1,2,0:T(8,128)S(1)}, f32[16,255]{1,0:T(8,128)S(1)}, bf16[16,4096]{1,0:T(8,128)(2,1)S(1)}, s32[]{:T(128)}, /*index=5*...) while((s32[]{:T(128)}, f32[16,128,16]{1,2,0:T(8,128)S(1)}, ...), condition=%wide.region_5.4_spmd, body=%wide.region_3.3_spmd.sunk | while | flops 1081988 | bytes 1568901 | solution.py:73
  409.0 557.2 %reduce-scatter.2.cloned.1.call-done = f32[16,128]{1,0:T(8,128)} async-done(((f32[16,2048]{1,0:T(8,128)}), f32[16,128]{1,0:T(8,128)}) %reduce-scatter.2.cloned.1.call-update) | async-done | bytes 8208 | tf_op jit(solution)/shard_map/reduce_scatter | solution.py:111
  966.2 1.3 broadcast_multiply_fusion
  (2532 shorter events, 267.4 us)
Async XLA Ops:
  7.2 1.0 copy-start.1
  7.2 50.3 %all-gather.7.cloned.1.call-start = ((), (), s32[]{:S(2)}) async-start(), calls=%async_computation.3 | async-start | bytes 1114112 | tf_op jit(solution)/shard_map/all_gather | solution.py:86
  9.0 0.8 copy-start.2
  9.0 301.7 %all-gather.5.cloned.1.call-start = ((), (), s32[]{:S(2)}) async-start(), calls=%async_computation.2 | async-start | bytes 1114112 | tf_op jit(solution)/shard_map/all_gather | solution.py:56
  9.8 0.8 copy-start.3
  10.6 0.8 copy-start
  261.8 704.4 %reduce-scatter.2.cloned.1.call-start = ((), (), s32[]{:S(2)}) async-start(), calls=%async_computation.1 | async-start | bytes 139264 | tf_op jit(solution)/shard_map/reduce_scatter | solution.py:111
Sparse Core Ops, SparseCore 0:
  10.6 46.8 all-gather.6
  261.9 48.7 all-gather.4
  406.1 560.0 reduce-scatter.1
where the time goes:
time: 986 us; the launch traced here: 974 us
  waiting for transfers between devices  652 us (66%)
  local copies, waits for them, and re-layouts  187 us (19%)
  matrix products  63.3 us (6%)
  loops' own time  31.2 us (3%)
  other arithmetic  26.1 us (3%)
  between operations  13.9 us (1%)
    reduce_scatter x1, waiting for transfers between devices, on_device(): lax.psum_scatter(lag_full, 'seq', scatter_dimension=1, tiled=True)  557 us
    reshape x272, local copies, waits for them, and re-layouts, toeplitz(): return flat.reshape(width, 2 * width + 1)[:, :width][:, ::-1]  75.9 us
    all_gather x1, waiting for transfers between devices, on_device(): incoming = lax.all_gather(mixed_in[None], 'seq', axis=0, tiled=True)  48.9 us
    all_gather x1, waiting for transfers between devices, on_device(): incoming = lax.all_gather(grad_mix[None], 'seq', axis=0, tiled=True)  46 us
    dot_general x240, matrix products, backward_one_group(): jnp.einsum('ab,ag->bg', kern, grads, preferred_element_type=jnp.float32)  30.6 us
    dot_general x32, matrix products, forward_one_group(): jnp.einsum('ag,bg->ab', grads, source, preferred_element_type=jnp.float32)  28.7 us
    dynamic_slice x272, local copies, waits for them, and re-layouts, toeplitz(): segment = lax.dynamic_slice_in_dim(padded_row, begin_at, 2 * width - 1, 0)  27.7 us
    rev x272, local copies, waits for them, and re-layouts, toeplitz(): return flat.reshape(width, 2 * width + 1)[:, :width][:, ::-1]  25.3 us
  transfers between devices with their start and end apart: 3, of which 3 were waited for; matrix products, arithmetic and copies ran while one was open for 0% of the time, Pallas kernels for 0%

commit v1 on v0

v1 whole, which is shorter than its diff:
```python
import functools
import math

import jax
import jax.numpy as jnp
from jax import lax
from jax.experimental import pallas as pl
from jax.experimental.pallas import tpu as pltpu
from jax.sharding import PartitionSpec as P

GROUP = 16
F32 = jnp.float32
BF16 = jnp.bfloat16


def pack_kernel(post_ref, pre_ref, values_ref, gout_ref, send_ref):
    n_filters = send_ref.shape[0]
    tokens = post_ref.shape[0]
    mixed = pre_ref[...].astype(F32) * values_ref[...].astype(F32)
    grads = gout_ref[...].astype(F32) * post_ref[...].astype(F32)
    send_ref[:, 0:GROUP, :] = mixed.astype(BF16).T.reshape(n_filters, GROUP, tokens)
    send_ref[:, GROUP : 2 * GROUP, :] = grads.astype(BF16).T.reshape(n_filters, GROUP, tokens)


def conv_kernel(own_ref, recv_ref, filters_ref, back_ref):
    blocks, _, width = recv_ref.shape
    rows = blocks * GROUP
    length = blocks * width
    xt = recv_ref[:, 0:GROUP, :].reshape(rows, width)
    gt = recv_ref[:, GROUP : 2 * GROUP, :].reshape(rows, width)
    own = own_ref[0]
    taps = filters_ref[...].astype(F32)
    which = lax.broadcasted_iota(jnp.int32, taps.shape, 0)
    row = jnp.sum(jnp.where(which == own, taps, 0.0), axis=0, keepdims=True)
    padded = jnp.concatenate([jnp.zeros((1, width), F32), row], axis=1)
    toep = pltpu.roll(
        jnp.broadcast_to(padded, (width, length + width)), 0, 1, stride=1, stride_axis=0
    ).astype(BF16)

    filt = None
    back = None
    for d in range(blocks):
        kern = toep[:, width * (d + 1) : width * (d + 2)]
        part = jnp.dot(xt[: rows - GROUP * d], kern, preferred_element_type=F32)
        rev = lax.dot_general(
            gt[GROUP * d :], kern, (((1,), (1,)), ((), ())), preferred_element_type=F32
        )
        if d == 0:
            filt, back = part, rev
        else:
            zeros = jnp.zeros((GROUP * d, width), F32)
            filt = filt + jnp.concatenate([zeros, part], axis=0)
            back = back + jnp.concatenate([rev, zeros], axis=0)
    back_ref[:, 0:GROUP, :] = filt.astype(BF16).reshape(blocks, GROUP, width)
    back_ref[:, GROUP : 2 * GROUP, :] = back.astype(BF16).reshape(blocks, GROUP, width)

    at = lax.broadcasted_iota(jnp.int32, (width, width), 0)
    to = lax.broadcasted_iota(jnp.int32, (width, width), 1)
    flip = jnp.where(at + to == width - 1, 1.0, 0.0).astype(BF16)
    x_rev = lax.dot_general(
        flip, xt, (((1,), (1,)), ((), ())), preferred_element_type=F32
    ).astype(BF16)
    gt_pad = jnp.concatenate([gt, jnp.zeros((rows, width), BF16)], axis=0)
    pairs = [
        jnp.dot(x_rev, gt_pad[GROUP * d : GROUP * d + rows], preferred_element_type=F32)
        for d in range(blocks)
    ]
    pairs = jnp.concatenate(pairs + [jnp.zeros((width, width), F32)], axis=1)
    turned = pltpu.roll(pairs, 1, 1, stride=1, stride_axis=0)
    lags = jnp.sum(turned[:, width:], axis=0, keepdims=True)
    high = lags.astype(BF16).astype(F32)
    rest = lags - high
    mid = rest.astype(BF16).astype(F32)
    low = rest - mid
    terms = jnp.concatenate([high, mid, low, jnp.zeros((13, length), F32)], axis=0).astype(BF16)
    for i in range(blocks):
        back_ref[i, 2 * GROUP : 3 * GROUP, :] = terms[:, width * i : width * (i + 1)]


def gate_kernel(length, recv_ref, post_ref, pre_ref, values_ref, gout_ref, out_ref, gpost_ref, gpre_ref, gval_ref, gfilt_ref):
    n_filters, _, tokens = recv_ref.shape
    channels = n_filters * GROUP
    filt = recv_ref[:, 0:GROUP, :].reshape(channels, tokens).astype(F32).T
    back = recv_ref[:, GROUP : 2 * GROUP, :].reshape(channels, tokens).astype(F32).T
    out_ref[...] = (post_ref[...].astype(F32) * filt).astype(BF16)
    gpost_ref[...] = (gout_ref[...].astype(F32) * filt).astype(BF16)
    gpre_ref[...] = (back * values_ref[...].astype(F32)).astype(BF16)
    gval_ref[...] = (back * pre_ref[...].astype(F32)).astype(BF16)
    scale = 1.0 / math.sqrt(GROUP * length)
    terms = recv_ref[:, 2 * GROUP : 3 * GROUP, :].astype(F32)
    gfilt_ref[...] = jnp.sum(terms, axis=1) * scale


def on_device(post_gate, pre_gate, values_in, filters, grad_out):
    tokens, channels = post_gate.shape
    n_filters, length = filters.shape
    vmem = pl.BlockSpec(memory_space=pltpu.VMEM)
    smem = pl.BlockSpec(memory_space=pltpu.SMEM)
    send = pl.pallas_call(
        pack_kernel,
        out_shape=jax.ShapeDtypeStruct((n_filters, 2 * GROUP, tokens), BF16),
        in_specs=[vmem] * 4,
        out_specs=vmem,
        name="pack",
    )(post_gate, pre_gate, values_in, grad_out)
    recv = lax.all_to_all(send, "seq", 0, 0, tiled=True)
    own = lax.axis_index("seq").astype(jnp.int32).reshape(1)
    back = pl.pallas_call(
        conv_kernel,
        out_shape=jax.ShapeDtypeStruct((n_filters, 3 * GROUP, tokens), BF16),
        in_specs=[smem, vmem, vmem],
        out_specs=vmem,
        name="conv",
    )(own, recv, filters)
    back = lax.all_to_all(back, "seq", 0, 0, tiled=True)
    grid_out = jax.ShapeDtypeStruct((tokens, channels), BF16)
    return pl.pallas_call(
        functools.partial(gate_kernel, length),
        out_shape=(grid_out,) * 4 + (jax.ShapeDtypeStruct((n_filters, tokens), F32),),
        in_specs=[vmem] * 5,
        out_specs=(vmem,) * 5,
        name="gate",
    )(back, post_gate, pre_gate, values_in, grad_out)


def solution(mesh):
    return jax.shard_map(
        on_device,
        mesh=mesh,
        in_specs=(
            P("seq", "grp"),
            P("seq", "grp"),
            P("seq", "grp"),
            P("grp", None),
            P("seq", "grp"),
        ),
        out_specs=(
            P("seq", "grp"),
            P("seq", "grp"),
            P("seq", "grp"),
            P("seq", "grp"),
            P("grp", "seq"),
        ),
        check_vma=False,
    )
```

time: 986 us -> 43 us (0.04); the launches traced: 974 us -> 42.6 us
  waiting for transfers between devices: 652 us -> 9.17 us
  local copies, waits for them, and re-layouts: 187 us -> 0.65 us
  matrix products: 63.3 us -> 0 us
  loops' own time: 31.2 us -> 0 us
  other arithmetic: 26.1 us -> 0 us
  blocking collectives: 0 us -> 13.9 us
  between operations: 13.9 us -> 0.63 us
  starting transfers between devices: 0.12 us -> 11.8 us
    reduce_scatter x1 -> x0, waiting for transfers between devices: 557 us -> none  [on_device(): lax.psum_scatter(lag_full, 'seq', scatter_dimension=1, tiled=True)]
    all_gather x2 -> x0, waiting for transfers between devices: 94.9 us -> none  [the longest x1 48.9 us: on_device(): incoming = lax.all_gather(mixed_in[None], 'seq', axis=0, tiled=True)]
    reshape x304 -> x0, local copies, waits for them, and re-layouts: 86.5 us -> none  [the longest x272 75.9 us: toeplitz(): return flat.reshape(width, 2 * width + 1)[:, :width][:, ::-1]]
    dot_general x304 -> x0, matrix products: 63.3 us -> none  [the longest x240 30.6 us: backward_one_group(): jnp.einsum('ab,ag->bg', kern, grads, preferred_element_type=jnp.float32)]
    dynamic_slice x323 -> x0, local copies, waits for them, and re-layouts: 46.7 us -> none  [the longest x272 27.7 us: toeplitz(): segment = lax.dynamic_slice_in_dim(padded_row, begin_at, 2 * width - 1, 0)]
    another operation x51 -> x0, loops' own time: 31.2 us -> none  [the longest x1 10.9 us: on_device(): lax.scan(forward_one_shard, (zero_filt, zero_dist), (incoming, jnp.arange...]
    rev x304 -> x0, local copies, waits for them, and re-layouts: 27.8 us -> none  [the longest x272 25.3 us: toeplitz(): return flat.reshape(width, 2 * width + 1)[:, :width][:, ::-1]]
    concatenate x272 -> x0, other arithmetic: 21 us -> none  [toeplitz(): extended = jnp.concatenate([segment, jnp.zeros((1,), segment.dtype)])]
  transfers between devices with their start and end apart: 3 -> 1, of which waited for: 3 -> 1; matrix products, arithmetic and copies ran while one was open for 0% -> 0% of each run, Pallas kernels for 0% -> 0%
where the time goes in v1:
time: 43 us; the launch traced here: 42.6 us
  blocking collectives  13.9 us (32%)
  starting transfers between devices  11.8 us (27%)
  waiting for transfers between devices  9.17 us (21%)
  Pallas kernels  6.42 us (15%)
  local copies, waits for them, and re-layouts  0.65 us (2%)
  between operations  0.63 us (1%)
    all_to_all x1, blocking collectives, on_device(): back = lax.all_to_all(back, 'seq', 0, 0, tiled=True)  13.9 us
    all_to_all x1, starting transfers between devices, on_device(): recv = lax.all_to_all(send, 'seq', 0, 0, tiled=True)  11.8 us
    all_to_all x1, waiting for transfers between devices, on_device(): recv = lax.all_to_all(send, 'seq', 0, 0, tiled=True)  9.17 us
    pallas_call x1, Pallas kernels, on_device(): pl.pallas_call(conv_kernel, out_shape=jax.ShapeDtypeStruct((n_filters, 3...  2.9 us
    pallas_call x1, Pallas kernels, on_device(): pl.pallas_call(functools.partial(gate_kernel, length), out_shape=(grid_ou...  1.85 us
    pallas_call x1, Pallas kernels, on_device(): pl.pallas_call(pack_kernel, out_shape=jax.ShapeDtypeStruct((n_filters, 2...  1.68 us
  transfers between devices with their start and end apart: 1, of which 1 were waited for; matrix products, arithmetic and copies ran while one was open for 0% of the time, Pallas kernels for 0%

profile of v1, /device:TPU:1, one launch (start us, length us, event | category | flops | bytes accessed | tf_op | source)
XLA Modules:
  0.0 42.6 jit_solution(18025647938835144)
XLA Ops:
  0.6 1.7 %pack.1 = bf16[16,32,128]{2,1,0:T(8,128)(2,1)} custom-call(bf16[128,256]{1,0:T(8,128)(2,1)} %post_ref.3, bf16[128,256]{1,0:T(8,128)(2,1)} %pre_ref.3, bf16[128,256]{1,0:T(8,128)(2,1)} %values_ref.3, bf16[128,256]{1,0:T(8,128)(2,1)} %gout_ref.3), custom_call_target="tpu_custom_call" | custom-call | tf_op jit(solution)/shard_map/pack/pallas_call | solution.py:99
  2.3 11.8 %all-to-all-start = ((bf16[16,32,128]{2,1,0:T(8,128)(2,1)}), bf16[16,32,128]{2,1,0:T(8,128)(2,1)S(1)}, u32[]{:S(2)}, u32[]{:S(2)}) async-start(bf16[16,32,128]{2,1,0:T(8,128)(2,1)} %pack.1), calls=%async_computation | async-start | bytes 262144 | tf_op jit(solution)/shard_map/all_to_all | solution.py:106
  14.1 9.2 %all-to-all-done.recv_ref = bf16[16,32,128]{2,1,0:T(8,128)(2,1)S(1)} async-done(((bf16[16,32,128]{2,1,0:T(8,128)(2,1)}), bf16[16,32,128]{2,1,0:T(8,128)(2,1)S(1)}, u32[]{:S(2)}, u32[]{:S(2)}) %all-to-all-start) | async-done | bytes 131104 | tf_op jit(solution)/shard_map/all_to_all | solution.py:106
  23.3 0.0 copy-start
  23.3 0.6 %copy-done = bf16[16,32,128]{2,1,0:T(8,128)(2,1)} copy-done((bf16[16,32,128]{2,1,0:T(8,128)(2,1)}, bf16[16,32,128]{2,1,0:T(8,128)(2,1)S(1)}, u32[]{:S(2)}) %copy-start) | copy-done | bytes 131096
  24.0 2.9 %conv.1 = bf16[16,48,128]{2,1,0:T(8,128)(2,1)} custom-call(s32[1]{0:T(128)} %bitcast.own_ref, bf16[16,32,128]{2,1,0:T(8,128)(2,1)} %copy-done, bf16[16,2048]{1,0:T(8,128)(2,1)} %filters_ref.1), custom_call_target="tpu_custom_call" | custom-call | tf_op jit(solution)/shard_map/conv/pallas_call | solution.py:108
  26.9 13.9 %all_to_all.10.recv_ref = bf16[16,48,128]{2,1,0:T(8,128)(2,1)} all-to-all(bf16[16,48,128]{2,1,0:T(8,128)(2,1)} %conv.1), channel_id=1, replica_groups=mesh['seq'=16,'grp'=32] {'seq'}, dimensions={0} | all-to-all | bytes 393216 | tf_op jit(solution)/shard_map/all_to_all | solution.py:115
  40.8 1.8 %gate.1 = (bf16[128,256]{1,0:T(8,128)(2,1)}, bf16[128,256]{1,0:T(8,128)(2,1)}, bf16[128,256]{1,0:T(8,128)(2,1)}, bf16[128,256]{1,0:T(8,128)(2,1)}, f32[16,128]{1,0:T(8,128)}) custom-call(bf16[16,48,128]{2,1,0:T(8,128)(2,1)} %all_to_all.10.recv_ref, bf16[128,256]{1,0:T(8,128)(2,1)} %post_ref.3, bf16[128,256]{1,0:T(8,128)(2,1)} %pre_ref.3, ...), custom_call_target="tpu_custom_call" | custom-call | tf_op jit(solution)/shard_map/gate/pallas_call | solution.py:117
Async XLA Ops:
  2.3 21.0 %all-to-all-start = ((bf16[16,32,128]{2,1,0:T(8,128)(2,1)}), bf16[16,32,128]{2,1,0:T(8,128)(2,1)S(1)}, u32[]{:S(2)}, u32[]{:S(2)}) async-start(bf16[16,32,128]{2,1,0:T(8,128)(2,1)} %pack.1), calls=%async_computation | async-start | bytes 262144 | tf_op jit(solution)/shard_map/all_to_all | solution.py:106
  23.3 0.7 %copy-start = (bf16[16,32,128]{2,1,0:T(8,128)(2,1)}, bf16[16,32,128]{2,1,0:T(8,128)(2,1)S(1)}, u32[]{:S(2)}) copy-start(bf16[16,32,128]{2,1,0:T(8,128)(2,1)S(1)} %all-to-all-done.recv_ref) | copy-start | bytes 393220

commit v2 on v1

--- a/solution.py
+++ b/solution.py
@@ -11,24 +11,33 @@
 GROUP = 16
 F32 = jnp.float32
 BF16 = jnp.bfloat16
+VMEM = 8 * 1024 * 1024
 
 
-def pack_kernel(post_ref, pre_ref, values_ref, gout_ref, send_ref):
-    n_filters = send_ref.shape[0]
-    tokens = post_ref.shape[0]
-    mixed = pre_ref[...].astype(F32) * values_ref[...].astype(F32)
-    grads = gout_ref[...].astype(F32) * post_ref[...].astype(F32)
-    send_ref[:, 0:GROUP, :] = mixed.astype(BF16).T.reshape(n_filters, GROUP, tokens)
-    send_ref[:, GROUP : 2 * GROUP, :] = grads.astype(BF16).T.reshape(n_filters, GROUP, tokens)
+def pack_kernel(post_hbm, pre_hbm, values_hbm, gout_hbm, send_ref, held, sems):
+    n_filters, _, tokens = send_ref.shape
+    copies = [
+        pltpu.make_async_copy(hbm, held.at[k], sems.at[k])
+        for k, hbm in enumerate((pre_hbm, values_hbm, gout_hbm, post_hbm))
+    ]
+    for copy in copies:
+        copy.start()
+    for k in range(2):
+        copies[2 * k].wait()
+        copies[2 * k + 1].wait()
+        product = held[2 * k].astype(F32) * held[2 * k + 1].astype(F32)
+        send_ref[:, GROUP * k : GROUP * (k + 1), :] = product.astype(BF16).T.reshape(
+            n_filters, GROUP, tokens
+        )
 
 
-def conv_kernel(own_ref, recv_ref, filters_ref, back_ref):
+def conv_kernel(recv_ref, filters_ref, back_ref):
     blocks, _, width = recv_ref.shape
     rows = blocks * GROUP
     length = blocks * width
     xt = recv_ref[:, 0:GROUP, :].reshape(rows, width)
     gt = recv_ref[:, GROUP : 2 * GROUP, :].reshape(rows, width)
-    own = own_ref[0]
+    own = lax.axis_index("seq")
     taps = filters_ref[...].astype(F32)
     which = lax.broadcasted_iota(jnp.int32, taps.shape, 0)
     row = jnp.sum(jnp.where(which == own, taps, 0.0), axis=0, keepdims=True)
@@ -95,23 +104,28 @@
     tokens, channels = post_gate.shape
     n_filters, length = filters.shape
     vmem = pl.BlockSpec(memory_space=pltpu.VMEM)
-    smem = pl.BlockSpec(memory_space=pltpu.SMEM)
+    hbm = pl.BlockSpec(memory_space=pltpu.HBM)
     send = pl.pallas_call(
         pack_kernel,
         out_shape=jax.ShapeDtypeStruct((n_filters, 2 * GROUP, tokens), BF16),
-        in_specs=[vmem] * 4,
+        in_specs=[hbm] * 4,
         out_specs=vmem,
+        scratch_shapes=[
+            pltpu.VMEM((4, tokens, channels), BF16),
+            pltpu.SemaphoreType.DMA((4,)),
+        ],
+        compiler_params=pltpu.CompilerParams(vmem_limit_bytes=VMEM),
         name="pack",
-    )(post_gate, pre_gate, values_in, grad_out)
+    )(*[pltpu.with_memory_space_constraint(x, pltpu.HBM) for x in (post_gate, pre_gate, values_in, grad_out)])
     recv = lax.all_to_all(send, "seq", 0, 0, tiled=True)
-    own = lax.axis_index("seq").astype(jnp.int32).reshape(1)
     back = pl.pallas_call(
         conv_kernel,
         out_shape=jax.ShapeDtypeStruct((n_filters, 3 * GROUP, tokens), BF16),
-        in_specs=[smem, vmem, vmem],
+        in_specs=[vmem, vmem],
         out_specs=vmem,
+        compiler_params=pltpu.CompilerParams(vmem_limit_bytes=VMEM),
         name="conv",
-    )(own, recv, filters)
+    )(recv, filters)
     back = lax.all_to_all(back, "seq", 0, 0, tiled=True)
     grid_out = jax.ShapeDtypeStruct((tokens, channels), BF16)
     return pl.pallas_call(
@@ -119,6 +133,7 @@
         out_shape=(grid_out,) * 4 + (jax.ShapeDtypeStruct((n_filters, tokens), F32),),
         in_specs=[vmem] * 5,
         out_specs=(vmem,) * 5,
+        compiler_params=pltpu.CompilerParams(vmem_limit_bytes=VMEM),
         name="gate",
     )(back, post_gate, pre_gate, values_in, grad_out)
 

time: 43 us -> 38 us (0.88)
  blocking collectives: 13.9 us -> 33.8 us
  starting transfers between devices: 11.8 us -> 0 us
  waiting for transfers between devices: 9.17 us -> 0 us
  Pallas kernels: 6.42 us -> 3.19 us
  local copies, waits for them, and re-layouts: 0.65 us -> 0.03 us
    all_to_all x0 -> x1, blocking collectives: none -> 20.9 us  [on_device(): recv = lax.all_to_all(send, 'seq', 0, 0, tiled=True)]
    all_to_all x1 -> x0, starting transfers between devices: 11.8 us -> none  [on_device(): recv = lax.all_to_all(send, 'seq', 0, 0, tiled=True)]
    all_to_all x1 -> x0, waiting for transfers between devices: 9.17 us -> none  [on_device(): recv = lax.all_to_all(send, 'seq', 0, 0, tiled=True)]
    pallas_call x1, Pallas kernels: 2.9 us -> 1.3 us  [on_device(): pl.pallas_call(conv_kernel, out_shape=jax.ShapeDtypeStruct((n_filters, 3...]
    all_to_all x1, blocking collectives: 13.9 us -> 12.9 us  [on_device(): back = lax.all_to_all(back, 'seq', 0, 0, tiled=True)]
    pallas_call x1, Pallas kernels: 1.85 us -> 0.82 us  [on_device(): pl.pallas_call(functools.partial(gate_kernel, length), out_shape=(grid_ou...]
    unnamed x2 -> x10, local copies, waits for them, and re-layouts: 0.65 us -> 0.03 us
    pallas_call x1, Pallas kernels: 1.68 us -> 1.06 us  [on_device(): pl.pallas_call(pack_kernel, out_shape=jax.ShapeDtypeStruct((n_filters, 2...]
  transfers between devices with their start and end apart: 1 -> 0, of which waited for: 1 -> 0; matrix products, arithmetic and copies ran while one was open for 0% -> 0% of each run, Pallas kernels for 0% -> 0%
where the time goes in v2:
time: 38 us; the launch traced here: 37.7 us
  blocking collectives  33.8 us (89%)
  Pallas kernels  3.19 us (8%)
  between operations  0.69 us (2%)
    all_to_all x1, blocking collectives, on_device(): recv = lax.all_to_all(send, 'seq', 0, 0, tiled=True)  20.9 us
    all_to_all x1, blocking collectives, on_device(): back = lax.all_to_all(back, 'seq', 0, 0, tiled=True)  12.9 us
    pallas_call x1, Pallas kernels, on_device(): pl.pallas_call(conv_kernel, out_shape=jax.ShapeDtypeStruct((n_filters, 3...  1.3 us
    pallas_call x1, Pallas kernels, on_device(): pl.pallas_call(pack_kernel, out_shape=jax.ShapeDtypeStruct((n_filters, 2...  1.06 us
    pallas_call x1, Pallas kernels, on_device(): pl.pallas_call(functools.partial(gate_kernel, length), out_shape=(grid_ou...  0.82 us

profile of v2, /device:TPU:1, one launch (start us, length us, event | category | flops | bytes accessed | tf_op | source)
XLA Modules:
  0.0 37.7 jit_solution(10764002509206866773)
XLA Ops:
  0.6 1.1 %pack.1 = bf16[16,32,128]{2,1,0:T(8,128)(2,1)S(1)} custom-call(bf16[128,256]{1,0:T(8,128)(2,1)} %post_ref.1, bf16[128,256]{1,0:T(8,128)(2,1)} %pre_ref.1, bf16[128,256]{1,0:T(8,128)(2,1)} %values_ref.1, bf16[128,256]{1,0:T(8,128)(2,1)} %gout_ref.1), custom_call_target="tpu_custom_call" | custom-call | tf_op jit(solution)/shard_map/pack/pallas_call | solution.py:108
  1.7 0.0 copy-start.4
  1.7 20.9 %all_to_all.10.recv_ref = bf16[16,32,128]{2,1,0:T(8,128)(2,1)S(1)} all-to-all(bf16[16,32,128]{2,1,0:T(8,128)(2,1)S(1)} %pack.1), channel_id=1, replica_groups=mesh['seq'=16,'grp'=32] {'seq'}, dimensions={0} | all-to-all | bytes 262144 | tf_op jit(solution)/shard_map/all_to_all | solution.py:120
  22.6 0.0 copy-done.4
  22.6 1.3 %conv.1 = bf16[16,48,128]{2,1,0:T(8,128)(2,1)S(1)} custom-call(bf16[16,32,128]{2,1,0:T(8,128)(2,1)S(1)} %all_to_all.10.recv_ref, bf16[16,2048]{1,0:T(8,128)(2,1)S(1)} %copy-done.4), custom_call_target="tpu_custom_call" | custom-call | tf_op jit(solution)/shard_map/conv/pallas_call | solution.py:121
  23.9 0.0 copy-start
  24.0 0.0 copy-start.1
  24.0 0.0 copy-start.2
  24.0 0.0 copy-start.3
  24.0 12.9 %all_to_all.11.recv_ref = bf16[16,48,128]{2,1,0:T(8,128)(2,1)S(1)} all-to-all(bf16[16,48,128]{2,1,0:T(8,128)(2,1)S(1)} %conv.1), channel_id=1, replica_groups=mesh['seq'=16,'grp'=32] {'seq'}, dimensions={0} | all-to-all | bytes 393216 | tf_op jit(solution)/shard_map/all_to_all | solution.py:129
  36.9 0.0 copy-done
  36.9 0.0 copy-done.1
  36.9 0.0 copy-done.2
  36.9 0.0 copy-done.3
  36.9 0.8 %gate.1 = (bf16[128,256]{1,0:T(8,128)(2,1)}, bf16[128,256]{1,0:T(8,128)(2,1)}, bf16[128,256]{1,0:T(8,128)(2,1)}, bf16[128,256]{1,0:T(8,128)(2,1)}, f32[16,128]{1,0:T(8,128)}) custom-call(bf16[16,48,128]{2,1,0:T(8,128)(2,1)S(1)} %all_to_all.11.recv_ref, bf16[128,256]{1,0:T(8,128)(2,1)S(1)} %copy-done, bf16[128,256]{1,0:T(8,128)(2,1)S(1)} %copy-done.1, ...), custom_call_target="tpu_custom_call" | custom-call | tf_op jit(solution)/shard_map/gate/pallas_call | solution.py:131
Async XLA Ops:
  1.7 20.9 %copy-start.4 = (bf16[16,2048]{1,0:T(8,128)(2,1)S(1)}, bf16[16,2048]{1,0:T(8,128)(2,1)}, u32[]{:S(2)}) copy-start(bf16[16,2048]{1,0:T(8,128)(2,1)} %filters_ref.1) | copy-start | bytes 196612
  23.9 12.9 %copy-start = (bf16[128,256]{1,0:T(8,128)(2,1)S(1)}, bf16[128,256]{1,0:T(8,128)(2,1)}, u32[]{:S(2)}) copy-start(bf16[128,256]{1,0:T(8,128)(2,1)} %post_ref.1) | copy-start | bytes 196612
  24.0 12.9 %copy-start.1 = (bf16[128,256]{1,0:T(8,128)(2,1)S(1)}, bf16[128,256]{1,0:T(8,128)(2,1)}, u32[]{:S(2)}) copy-start(bf16[128,256]{1,0:T(8,128)(2,1)} %pre_ref.1) | copy-start | bytes 196612
  24.0 12.9 %copy-start.2 = (bf16[128,256]{1,0:T(8,128)(2,1)S(1)}, bf16[128,256]{1,0:T(8,128)(2,1)}, u32[]{:S(2)}) copy-start(bf16[128,256]{1,0:T(8,128)(2,1)} %values_ref.1) | copy-start | bytes 196612
  24.0 12.9 %copy-start.3 = (bf16[128,256]{1,0:T(8,128)(2,1)S(1)}, bf16[128,256]{1,0:T(8,128)(2,1)}, u32[]{:S(2)}) copy-start(bf16[128,256]{1,0:T(8,128)(2,1)} %gout_ref.1) | copy-start | bytes 196612

commit v3 on v2

v3 whole, which is shorter than its diff:
```python
import functools
import math

import jax
import jax.numpy as jnp
from jax import lax
from jax.experimental import pallas as pl
from jax.experimental.pallas import tpu as pltpu
from jax.sharding import PartitionSpec as P

GROUP = 16
BACK_ROWS = 2 * GROUP + 8
F32 = jnp.float32
BF16 = jnp.bfloat16
VMEM = 8 * 1024 * 1024


ORDER_IN = list(range(15, -1, -1))
ORDER_OUT = list(range(0, 16, 2)) + list(range(1, 16, 2))


def pack_kernel(post_hbm, pre_hbm, values_hbm, gout_hbm, send_ref, held, sems):
    copies = [
        pltpu.make_async_copy(hbm, held.at[k], sems.at[k])
        for k, hbm in enumerate((pre_hbm, values_hbm, gout_hbm, post_hbm))
    ]
    for copy in copies:
        copy.start()
    for k in range(2):
        copies[2 * k].wait()
        copies[2 * k + 1].wait()
        product = held[2 * k].astype(F32) * held[2 * k + 1].astype(F32)
        turned = product.astype(BF16).T
        for place, f in enumerate(ORDER_IN):
            send_ref[place, GROUP * k : GROUP * (k + 1), :] = turned[GROUP * f : GROUP * (f + 1)]


def conv_kernel(recv_ref, filters_ref, back_ref):
    blocks, _, width = recv_ref.shape
    rows = blocks * GROUP
    length = blocks * width
    places = [ORDER_IN.index(block) for block in range(blocks)]
    xt = jnp.concatenate([recv_ref[p, 0:GROUP, :] for p in places], axis=0)
    gt = jnp.concatenate([recv_ref[p, GROUP : 2 * GROUP, :] for p in places], axis=0)
    own = lax.axis_index("seq")
    taps = filters_ref[...].astype(F32)
    which = lax.broadcasted_iota(jnp.int32, taps.shape, 0)
    row = jnp.sum(jnp.where(which == own, taps, 0.0), axis=0, keepdims=True)
    padded = jnp.concatenate([jnp.zeros((1, width), F32), row], axis=1)
    toep = pltpu.roll(
        jnp.broadcast_to(padded, (width, length + width)), 0, 1, stride=1, stride_axis=0
    ).astype(BF16)

    def wide(v):
        v = v.reshape(blocks // 2, 2, GROUP, width)
        return jnp.concatenate([v[:, 0].reshape(half, width), v[:, 1].reshape(half, width)], axis=1)

    half = rows // 2
    x2 = wide(xt)
    g2 = wide(gt)
    filt2 = None
    back2 = None
    for d in range(blocks // 2):
        top = toep[:, width * (2 * d + 1) : width * (2 * d + 3)]
        if d == 0:
            low = jnp.concatenate([jnp.zeros((width, width), BF16), toep[:, width : 2 * width]], axis=1)
        else:
            low = toep[:, width * 2 * d : width * (2 * d + 2)]
        kern = jnp.concatenate([top, low], axis=0)
        part = jnp.dot(x2[: half - GROUP * d], kern, preferred_element_type=F32)
        rev = lax.dot_general(
            g2[GROUP * d :], kern, (((1,), (1,)), ((), ())), preferred_element_type=F32
        )
        if d == 0:
            filt2, back2 = part, rev
        else:
            zeros = jnp.zeros((GROUP * d, 2 * width), F32)
            filt2 = filt2 + jnp.concatenate([zeros, part], axis=0)
            back2 = back2 + jnp.concatenate([rev, zeros], axis=0)
    filt2 = filt2.astype(BF16)
    back2 = back2.astype(BF16)
    for place, i in enumerate(ORDER_OUT):
        at = (slice(GROUP * (i // 2), GROUP * (i // 2 + 1)), slice(width * (i % 2), width * (i % 2 + 1)))
        back_ref[place, 0:GROUP, :] = filt2[at]
        back_ref[place, GROUP : 2 * GROUP, :] = back2[at]

    at = lax.broadcasted_iota(jnp.int32, (width, width), 0)
    to = lax.broadcasted_iota(jnp.int32, (width, width), 1)
    flip = jnp.where(at + to == width - 1, 1.0, 0.0).astype(BF16)
    x_rev = lax.dot_general(
        flip, xt, (((1,), (1,)), ((), ())), preferred_element_type=F32
    ).astype(BF16)
    gt_pad = jnp.concatenate([gt, jnp.zeros((rows, width), BF16)], axis=0)
    pairs = [
        jnp.dot(
            x_rev,
            jnp.concatenate(
                [gt_pad[GROUP * d : GROUP * d + rows], gt_pad[GROUP * (d + 1) : GROUP * (d + 1) + rows]],
                axis=1,
            ),
            preferred_element_type=F32,
        )
        for d in range(0, blocks, 2)
    ]
    pairs = jnp.concatenate(pairs + [jnp.zeros((width, width), F32)], axis=1)
    turned = pltpu.roll(pairs, 1, 1, stride=1, stride_axis=0)
    lags = jnp.sum(turned[:, width:], axis=0, keepdims=True)
    high = lags.astype(BF16).astype(F32)
    rest = lags - high
    mid = rest.astype(BF16).astype(F32)
    low = rest - mid
    terms = jnp.concatenate([high, mid, low, jnp.zeros((5, length), F32)], axis=0).astype(BF16)
    for place, i in enumerate(ORDER_OUT):
        back_ref[place, 2 * GROUP : BACK_ROWS, :] = terms[:, width * i : width * (i + 1)]


def gate_kernel(length, recv_ref, post_ref, pre_ref, values_ref, gout_ref, out_ref, gpost_ref, gpre_ref, gval_ref, gfilt_ref):
    n_filters = recv_ref.shape[0]
    places = [ORDER_OUT.index(f) for f in range(n_filters)]
    filt = jnp.concatenate([recv_ref[p, 0:GROUP, :] for p in places], axis=0).astype(F32).T
    back = jnp.concatenate([recv_ref[p, GROUP : 2 * GROUP, :] for p in places], axis=0).astype(F32).T
    out_ref[...] = (post_ref[...].astype(F32) * filt).astype(BF16)
    gpost_ref[...] = (gout_ref[...].astype(F32) * filt).astype(BF16)
    gpre_ref[...] = (back * values_ref[...].astype(F32)).astype(BF16)
    gval_ref[...] = (back * pre_ref[...].astype(F32)).astype(BF16)
    scale = 1.0 / math.sqrt(GROUP * length)
    lags = [
        jnp.sum(recv_ref[p, 2 * GROUP : BACK_ROWS, :].astype(F32), axis=0, keepdims=True)
        for p in places
    ]
    gfilt_ref[...] = jnp.concatenate(lags, axis=0) * scale


def on_device(post_gate, pre_gate, values_in, filters, grad_out):
    tokens, channels = post_gate.shape
    n_filters, length = filters.shape
    vmem = pl.BlockSpec(memory_space=pltpu.VMEM)
    hbm = pl.BlockSpec(memory_space=pltpu.HBM)
    send = pl.pallas_call(
        pack_kernel,
        out_shape=jax.ShapeDtypeStruct((n_filters, 2 * GROUP, tokens), BF16),
        in_specs=[hbm] * 4,
        out_specs=vmem,
        scratch_shapes=[
            pltpu.VMEM((4, tokens, channels), BF16),
            pltpu.SemaphoreType.DMA((4,)),
        ],
        compiler_params=pltpu.CompilerParams(vmem_limit_bytes=VMEM),
        name="pack",
    )(*[pltpu.with_memory_space_constraint(x, pltpu.HBM) for x in (post_gate, pre_gate, values_in, grad_out)])
    recv = lax.all_to_all(
        send, "seq", 0, 0, tiled=True, axis_index_groups=[ORDER_IN]
    )
    back = pl.pallas_call(
        conv_kernel,
        out_shape=jax.ShapeDtypeStruct((n_filters, BACK_ROWS, tokens), BF16),
        in_specs=[vmem, vmem],
        out_specs=vmem,
        compiler_params=pltpu.CompilerParams(vmem_limit_bytes=VMEM),
        name="conv",
    )(recv, filters)
    back = lax.all_to_all(
        back, "seq", 0, 0, tiled=True, axis_index_groups=[ORDER_OUT]
    )
    grid_out = jax.ShapeDtypeStruct((tokens, channels), BF16)
    return pl.pallas_call(
        functools.partial(gate_kernel, length),
        out_shape=(grid_out,) * 4 + (jax.ShapeDtypeStruct((n_filters, tokens), F32),),
        in_specs=[vmem] * 5,
        out_specs=(vmem,) * 5,
        compiler_params=pltpu.CompilerParams(vmem_limit_bytes=VMEM),
        name="gate",
    )(back, post_gate, pre_gate, values_in, grad_out)


def solution(mesh):
    return jax.shard_map(
        on_device,
        mesh=mesh,
        in_specs=(
            P("seq", "grp"),
            P("seq", "grp"),
            P("seq", "grp"),
            P("grp", None),
            P("seq", "grp"),
        ),
        out_specs=(
            P("seq", "grp"),
            P("seq", "grp"),
            P("seq", "grp"),
            P("seq", "grp"),
            P("grp", "seq"),
        ),
        check_vma=False,
    )
```

time: 38 us -> 35 us (0.921)
  blocking collectives: 33.8 us -> 31.1 us
    all_to_all x2, blocking collectives: 33.8 us -> 31.1 us  [the longest x1 18.6 us: on_device(): lax.all_to_all(send, 'seq', 0, 0, tiled=True, axis_index_groups=[ORDER_IN])]
where the time goes in v3:
time: 35 us; the launch traced here: 34.7 us
  blocking collectives  31.1 us (89%)
  Pallas kernels  2.91 us (8%)
  between operations  0.7 us (2%)
    all_to_all x1, blocking collectives, on_device(): lax.all_to_all(send, 'seq', 0, 0, tiled=True, axis_index_groups=[ORDER_IN])  18.6 us
    all_to_all x1, blocking collectives, on_device(): lax.all_to_all(back, 'seq', 0, 0, tiled=True, axis_index_groups=[ORDER_OUT])  12.5 us
    pallas_call x1, Pallas kernels, on_device(): pl.pallas_call(pack_kernel, out_shape=jax.ShapeDtypeStruct((n_filters, 2...  1.06 us
    pallas_call x1, Pallas kernels, on_device(): pl.pallas_call(conv_kernel, out_shape=jax.ShapeDtypeStruct((n_filters, BA...  1.02 us
    pallas_call x1, Pallas kernels, on_device(): pl.pallas_call(functools.partial(gate_kernel, length), out_shape=(grid_ou...  0.82 us

profile of v3, /device:TPU:1, one launch (start us, length us, event | category | flops | bytes accessed | tf_op | source)
XLA Modules:
  0.0 34.7 jit_solution(9980588102219595517)
XLA Ops:
  0.6 1.1 %pack.1 = bf16[16,32,128]{2,1,0:T(8,128)(2,1)S(1)} custom-call(bf16[128,256]{1,0:T(8,128)(2,1)} %post_ref.1, bf16[128,256]{1,0:T(8,128)(2,1)} %pre_ref.1, bf16[128,256]{1,0:T(8,128)(2,1)} %values_ref.1, bf16[128,256]{1,0:T(8,128)(2,1)} %gout_ref.1), custom_call_target="tpu_custom_call" | custom-call | tf_op jit(solution)/shard_map/pack/pallas_call | solution.py:139
  1.7 0.0 copy-start.4
  1.7 18.6 %all_to_all.10.recv_ref = bf16[16,32,128]{2,1,0:T(8,128)(2,1)S(1)} all-to-all(bf16[16,32,128]{2,1,0:T(8,128)(2,1)S(1)} %pack.1), channel_id=1, replica_groups={{480,448,416,384,352,320,288,256,224,192,160,128,96,64,32,0},{481,449,4..., dimensions={0} | all-to-all | bytes 262144 | tf_op jit(solution)/shard_map/all_to_all | solution.py:151
  20.3 0.0 copy-done.4
  20.3 1.0 %conv.1 = bf16[16,40,128]{2,1,0:T(8,128)(2,1)S(1)} custom-call(bf16[16,32,128]{2,1,0:T(8,128)(2,1)S(1)} %all_to_all.10.recv_ref, bf16[16,2048]{1,0:T(8,128)(2,1)S(1)} %copy-done.4), custom_call_target="tpu_custom_call" | custom-call | tf_op jit(solution)/shard_map/conv/pallas_call | solution.py:154
  21.4 0.0 copy-start
  21.4 0.0 copy-start.1
  21.4 0.0 copy-start.2
  21.4 0.0 copy-start.3
  21.4 12.5 %all_to_all.11.recv_ref = bf16[16,40,128]{2,1,0:T(8,128)(2,1)S(1)} all-to-all(bf16[16,40,128]{2,1,0:T(8,128)(2,1)S(1)} %conv.1), channel_id=1, replica_groups={{0,64,128,192,256,320,384,448,32,96,160,224,288,352,416,480},{1,65,129,..., dimensions={0} | all-to-all | bytes 327680 | tf_op jit(solution)/shard_map/all_to_all | solution.py:162
  33.9 0.0 copy-done
  33.9 0.0 copy-done.1
  33.9 0.0 copy-done.2
  33.9 0.0 copy-done.3
  33.9 0.8 %gate.1 = (bf16[128,256]{1,0:T(8,128)(2,1)}, bf16[128,256]{1,0:T(8,128)(2,1)}, bf16[128,256]{1,0:T(8,128)(2,1)}, bf16[128,256]{1,0:T(8,128)(2,1)}, f32[16,128]{1,0:T(8,128)}) custom-call(bf16[16,40,128]{2,1,0:T(8,128)(2,1)S(1)} %all_to_all.11.recv_ref, bf16[128,256]{1,0:T(8,128)(2,1)S(1)} %copy-done, bf16[128,256]{1,0:T(8,128)(2,1)S(1)} %copy-done.1, ...), custom_call_target="tpu_custom_call" | custom-call | tf_op jit(solution)/shard_map/gate/pallas_call | solution.py:166
Async XLA Ops:
  1.7 18.6 %copy-start.4 = (bf16[16,2048]{1,0:T(8,128)(2,1)S(1)}, bf16[16,2048]{1,0:T(8,128)(2,1)}, u32[]{:S(2)}) copy-start(bf16[16,2048]{1,0:T(8,128)(2,1)} %filters_ref.1) | copy-start | bytes 196612
  21.4 12.5 %copy-start = (bf16[128,256]{1,0:T(8,128)(2,1)S(1)}, bf16[128,256]{1,0:T(8,128)(2,1)}, u32[]{:S(2)}) copy-start(bf16[128,256]{1,0:T(8,128)(2,1)} %post_ref.1) | copy-start | bytes 196612
  21.4 12.5 %copy-start.1 = (bf16[128,256]{1,0:T(8,128)(2,1)S(1)}, bf16[128,256]{1,0:T(8,128)(2,1)}, u32[]{:S(2)}) copy-start(bf16[128,256]{1,0:T(8,128)(2,1)} %pre_ref.1) | copy-start | bytes 196612
  21.4 12.5 %copy-start.2 = (bf16[128,256]{1,0:T(8,128)(2,1)S(1)}, bf16[128,256]{1,0:T(8,128)(2,1)}, u32[]{:S(2)}) copy-start(bf16[128,256]{1,0:T(8,128)(2,1)} %values_ref.1) | copy-start | bytes 196612
  21.4 12.5 %copy-start.3 = (bf16[128,256]{1,0:T(8,128)(2,1)S(1)}, bf16[128,256]{1,0:T(8,128)(2,1)}, u32[]{:S(2)}) copy-start(bf16[128,256]{1,0:T(8,128)(2,1)} %gout_ref.1) | copy-start | bytes 196612

commit v4 on v3

--- a/solution.py
+++ b/solution.py
@@ -9,14 +9,14 @@
 from jax.sharding import PartitionSpec as P
 
 GROUP = 16
-BACK_ROWS = 2 * GROUP + 8
+BACK_PAIRS = GROUP + 1
 F32 = jnp.float32
 BF16 = jnp.bfloat16
 VMEM = 8 * 1024 * 1024
 
 
-ORDER_IN = list(range(15, -1, -1))
-ORDER_OUT = list(range(0, 16, 2)) + list(range(1, 16, 2))
+ORDER_IN = [13, 11, 9, 7, 5, 3, 1, 15, 12, 10, 8, 6, 4, 2, 0, 14]
+ORDER_OUT = [13, 15, 0, 2, 4, 6, 8, 10, 12, 14, 1, 3, 5, 7, 9, 11]
 
 
 def pack_kernel(post_hbm, pre_hbm, values_hbm, gout_hbm, send_ref, held, sems):
@@ -51,6 +51,32 @@
         jnp.broadcast_to(padded, (width, length + width)), 0, 1, stride=1, stride_axis=0
     ).astype(BF16)
 
+    at = lax.broadcasted_iota(jnp.int32, (width, width), 0)
+    to = lax.broadcasted_iota(jnp.int32, (width, width), 1)
+    flip = jnp.where(at + to == width - 1, 1.0, 0.0).astype(BF16)
+    x_rev = lax.dot_general(
+        flip, xt, (((1,), (1,)), ((), ())), preferred_element_type=F32
+    ).astype(BF16)
+    gt_pad = jnp.concatenate([gt, jnp.zeros((rows, width), BF16)], axis=0)
+    pairs = [
+        jnp.dot(
+            x_rev,
+            jnp.concatenate(
+                [gt_pad[GROUP * d : GROUP * d + rows], gt_pad[GROUP * (d + 1) : GROUP * (d + 1) + rows]],
+                axis=1,
+            ),
+            preferred_element_type=F32,
+        )
+        for d in range(0, blocks, 2)
+    ]
+    pairs = jnp.concatenate(pairs + [jnp.zeros((width, width), F32)], axis=1)
+    turned = pltpu.roll(pairs, 1, 1, stride=1, stride_axis=0)
+    lags = jnp.sum(turned[:, width:], axis=0, keepdims=True)
+    high = lags.astype(BF16).astype(F32)
+    terms = jnp.concatenate([high, lags - high], axis=0).astype(BF16)
+    for place, i in enumerate(ORDER_OUT):
+        back_ref[place, GROUP] = terms[:, width * i : width * (i + 1)]
+
     def wide(v):
         v = v.reshape(blocks // 2, 2, GROUP, width)
         return jnp.concatenate([v[:, 0].reshape(half, width), v[:, 1].reshape(half, width)], axis=1)
@@ -81,51 +107,28 @@
     back2 = back2.astype(BF16)
     for place, i in enumerate(ORDER_OUT):
         at = (slice(GROUP * (i // 2), GROUP * (i // 2 + 1)), slice(width * (i % 2), width * (i % 2 + 1)))
-        back_ref[place, 0:GROUP, :] = filt2[at]
-        back_ref[place, GROUP : 2 * GROUP, :] = back2[at]
-
-    at = lax.broadcasted_iota(jnp.int32, (width, width), 0)
-    to = lax.broadcasted_iota(jnp.int32, (width, width), 1)
-    flip = jnp.where(at + to == width - 1, 1.0, 0.0).astype(BF16)
-    x_rev = lax.dot_general(
-        flip, xt, (((1,), (1,)), ((), ())), preferred_element_type=F32
-    ).astype(BF16)
-    gt_pad = jnp.concatenate([gt, jnp.zeros((rows, width), BF16)], axis=0)
-    pairs = [
-        jnp.dot(
-            x_rev,
-            jnp.concatenate(
-                [gt_pad[GROUP * d : GROUP * d + rows], gt_pad[GROUP * (d + 1) : GROUP * (d + 1) + rows]],
-                axis=1,
-            ),
-            preferred_element_type=F32,
-        )
-        for d in range(0, blocks, 2)
-    ]
-    pairs = jnp.concatenate(pairs + [jnp.zeros((width, width), F32)], axis=1)
-    turned = pltpu.roll(pairs, 1, 1, stride=1, stride_axis=0)
-    lags = jnp.sum(turned[:, width:], axis=0, keepdims=True)
-    high = lags.astype(BF16).astype(F32)
-    rest = lags - high
-    mid = rest.astype(BF16).astype(F32)
-    low = rest - mid
-    terms = jnp.concatenate([high, mid, low, jnp.zeros((5, length), F32)], axis=0).astype(BF16)
-    for place, i in enumerate(ORDER_OUT):
-        back_ref[place, 2 * GROUP : BACK_ROWS, :] = terms[:, width * i : width * (i + 1)]
+        back_ref[place, 0 : GROUP // 2] = filt2[at].reshape(GROUP // 2, 2, width)
+        back_ref[place, GROUP // 2 : GROUP] = back2[at].reshape(GROUP // 2, 2, width)
 
 
 def gate_kernel(length, recv_ref, post_ref, pre_ref, values_ref, gout_ref, out_ref, gpost_ref, gpre_ref, gval_ref, gfilt_ref):
-    n_filters = recv_ref.shape[0]
+    n_filters, _, _, tokens = recv_ref.shape
     places = [ORDER_OUT.index(f) for f in range(n_filters)]
-    filt = jnp.concatenate([recv_ref[p, 0:GROUP, :] for p in places], axis=0).astype(F32).T
-    back = jnp.concatenate([recv_ref[p, GROUP : 2 * GROUP, :] for p in places], axis=0).astype(F32).T
+    filt, back = [
+        jnp.concatenate(
+            [recv_ref[p, half : half + GROUP // 2].reshape(GROUP, tokens) for p in places], axis=0
+        )
+        .astype(F32)
+        .T
+        for half in (0, GROUP // 2)
+    ]
     out_ref[...] = (post_ref[...].astype(F32) * filt).astype(BF16)
     gpost_ref[...] = (gout_ref[...].astype(F32) * filt).astype(BF16)
     gpre_ref[...] = (back * values_ref[...].astype(F32)).astype(BF16)
     gval_ref[...] = (back * pre_ref[...].astype(F32)).astype(BF16)
     scale = 1.0 / math.sqrt(GROUP * length)
     lags = [
-        jnp.sum(recv_ref[p, 2 * GROUP : BACK_ROWS, :].astype(F32), axis=0, keepdims=True)
+        jnp.sum(recv_ref[p, GROUP].astype(F32), axis=0, keepdims=True)
         for p in places
     ]
     gfilt_ref[...] = jnp.concatenate(lags, axis=0) * scale
@@ -153,7 +156,7 @@
     )
     back = pl.pallas_call(
         conv_kernel,
-        out_shape=jax.ShapeDtypeStruct((n_filters, BACK_ROWS, tokens), BF16),
+        out_shape=jax.ShapeDtypeStruct((n_filters, BACK_PAIRS, 2, tokens), BF16),
         in_specs=[vmem, vmem],
         out_specs=vmem,
         compiler_params=pltpu.CompilerParams(vmem_limit_bytes=VMEM),

time: 35 us -> 33.2 us (0.949)
  blocking collectives: 31.1 us -> 29.4 us
    all_to_all x1, blocking collectives: 12.5 us -> 11 us  [on_device(): lax.all_to_all(back, 'seq', 0, 0, tiled=True, axis_index_groups=[ORDER_OUT])]
where the time goes in v4:
time: 33.2 us; the launch traced here: 32.9 us
  blocking collectives  29.4 us (89%)
  Pallas kernels  2.8 us (8%)
  between operations  0.69 us (2%)
    all_to_all x1, blocking collectives, on_device(): lax.all_to_all(send, 'seq', 0, 0, tiled=True, axis_index_groups=[ORDER_IN])  18.4 us
    all_to_all x1, blocking collectives, on_device(): lax.all_to_all(back, 'seq', 0, 0, tiled=True, axis_index_groups=[ORDER_OUT])  11 us
    pallas_call x1, Pallas kernels, on_device(): pl.pallas_call(pack_kernel, out_shape=jax.ShapeDtypeStruct((n_filters, 2...  1.06 us
    pallas_call x1, Pallas kernels, on_device(): pl.pallas_call(conv_kernel, out_shape=jax.ShapeDtypeStruct((n_filters, BA...  0.88 us
    pallas_call x1, Pallas kernels, on_device(): pl.pallas_call(functools.partial(gate_kernel, length), out_shape=(grid_ou...  0.86 us

profile of v4, /device:TPU:1, one launch (start us, length us, event | category | flops | bytes accessed | tf_op | source)
XLA Modules:
  0.0 32.9 jit_solution(6726855358098143618)
XLA Ops:
  0.6 1.1 %pack.1 = bf16[16,32,128]{2,1,0:T(8,128)(2,1)S(1)} custom-call(bf16[128,256]{1,0:T(8,128)(2,1)} %post_ref.1, bf16[128,256]{1,0:T(8,128)(2,1)} %pre_ref.1, bf16[128,256]{1,0:T(8,128)(2,1)} %values_ref.1, bf16[128,256]{1,0:T(8,128)(2,1)} %gout_ref.1), custom_call_target="tpu_custom_call" | custom-call | tf_op jit(solution)/shard_map/pack/pallas_call | solution.py:142
  1.7 0.0 copy-start.4
  1.7 18.4 %all_to_all.10.recv_ref = bf16[16,32,128]{2,1,0:T(8,128)(2,1)S(1)} all-to-all(bf16[16,32,128]{2,1,0:T(8,128)(2,1)S(1)} %pack.1), channel_id=1, replica_groups={{416,352,288,224,160,96,32,480,384,320,256,192,128,64,0,448},{417,353,2..., dimensions={0} | all-to-all | bytes 262144 | tf_op jit(solution)/shard_map/all_to_all | solution.py:154
  20.1 0.0 copy-done.4
  20.1 0.9 %conv.1 = bf16[16,17,2,128]{3,2,1,0:T(2,128)(2,1)S(1)} custom-call(bf16[16,32,128]{2,1,0:T(8,128)(2,1)S(1)} %all_to_all.10.recv_ref, bf16[16,2048]{1,0:T(8,128)(2,1)S(1)} %copy-done.4), custom_call_target="tpu_custom_call" | custom-call | tf_op jit(solution)/shard_map/conv/pallas_call | solution.py:157
  21.0 0.0 copy-start
  21.0 0.0 copy-start.1
  21.0 0.0 copy-start.2
  21.0 0.0 copy-start.3
  21.1 11.0 %all_to_all.11.recv_ref = bf16[16,17,2,128]{3,2,1,0:T(2,128)(2,1)S(1)} all-to-all(bf16[16,17,2,128]{3,2,1,0:T(2,128)(2,1)S(1)} %conv.1), channel_id=1, replica_groups={{416,480,0,64,128,192,256,320,384,448,32,96,160,224,288,352},{417,481,1..., dimensions={0} | all-to-all | bytes 278528 | tf_op jit(solution)/shard_map/all_to_all | solution.py:165
  32.1 0.0 copy-done
  32.1 0.0 copy-done.1
  32.1 0.0 copy-done.2
  32.1 0.0 copy-done.3
  32.1 0.9 %gate.1 = (bf16[128,256]{1,0:T(8,128)(2,1)}, bf16[128,256]{1,0:T(8,128)(2,1)}, bf16[128,256]{1,0:T(8,128)(2,1)}, bf16[128,256]{1,0:T(8,128)(2,1)}, f32[16,128]{1,0:T(8,128)}) custom-call(bf16[16,17,2,128]{3,2,1,0:T(2,128)(2,1)S(1)} %all_to_all.11.recv_ref, bf16[128,256]{1,0:T(8,128)(2,1)S(1)} %copy-done, bf16[128,256]{1,0:T(8,128)(2,1)S(1)} %copy-done.1, ...), custom_call_target="tpu_custom_call" | custom-call | tf_op jit(solution)/shard_map/gate/pallas_call | solution.py:169
Async XLA Ops:
  1.7 18.4 %copy-start.4 = (bf16[16,2048]{1,0:T(8,128)(2,1)S(1)}, bf16[16,2048]{1,0:T(8,128)(2,1)}, u32[]{:S(2)}) copy-start(bf16[16,2048]{1,0:T(8,128)(2,1)} %filters_ref.1) | copy-start | bytes 196612
  21.0 11.1 %copy-start = (bf16[128,256]{1,0:T(8,128)(2,1)S(1)}, bf16[128,256]{1,0:T(8,128)(2,1)}, u32[]{:S(2)}) copy-start(bf16[128,256]{1,0:T(8,128)(2,1)} %post_ref.1) | copy-start | bytes 196612
  21.0 11.0 %copy-start.1 = (bf16[128,256]{1,0:T(8,128)(2,1)S(1)}, bf16[128,256]{1,0:T(8,128)(2,1)}, u32[]{:S(2)}) copy-start(bf16[128,256]{1,0:T(8,128)(2,1)} %pre_ref.1) | copy-start | bytes 196612
  21.0 11.0 %copy-start.2 = (bf16[128,256]{1,0:T(8,128)(2,1)S(1)}, bf16[128,256]{1,0:T(8,128)(2,1)}, u32[]{:S(2)}) copy-start(bf16[128,256]{1,0:T(8,128)(2,1)} %values_ref.1) | copy-start | bytes 196612
  21.0 11.0 %copy-start.3 = (bf16[128,256]{1,0:T(8,128)(2,1)S(1)}, bf16[128,256]{1,0:T(8,128)(2,1)}, u32[]{:S(2)}) copy-start(bf16[128,256]{1,0:T(8,128)(2,1)} %gout_ref.1) | copy-start | bytes 196612

commit v5 on v4

--- a/solution.py
+++ b/solution.py
@@ -15,7 +15,7 @@
 VMEM = 8 * 1024 * 1024
 
 
-ORDER_IN = [13, 11, 9, 7, 5, 3, 1, 15, 12, 10, 8, 6, 4, 2, 0, 14]
+ORDER_IN = [13, 14, 9, 7, 5, 3, 1, 15, 12, 10, 8, 6, 4, 2, 0, 11]
 ORDER_OUT = [13, 15, 0, 2, 4, 6, 8, 10, 12, 14, 1, 3, 5, 7, 9, 11]
 
 
@@ -84,25 +84,23 @@
     half = rows // 2
     x2 = wide(xt)
     g2 = wide(gt)
-    filt2 = None
-    back2 = None
+    kerns = []
     for d in range(blocks // 2):
         top = toep[:, width * (2 * d + 1) : width * (2 * d + 3)]
         if d == 0:
             low = jnp.concatenate([jnp.zeros((width, width), BF16), toep[:, width : 2 * width]], axis=1)
         else:
             low = toep[:, width * 2 * d : width * (2 * d + 2)]
-        kern = jnp.concatenate([top, low], axis=0)
-        part = jnp.dot(x2[: half - GROUP * d], kern, preferred_element_type=F32)
-        rev = lax.dot_general(
-            g2[GROUP * d :], kern, (((1,), (1,)), ((), ())), preferred_element_type=F32
-        )
-        if d == 0:
-            filt2, back2 = part, rev
-        else:
-            zeros = jnp.zeros((GROUP * d, 2 * width), F32)
-            filt2 = filt2 + jnp.concatenate([zeros, part], axis=0)
-            back2 = back2 + jnp.concatenate([rev, zeros], axis=0)
+        kerns.append(jnp.concatenate([top, low], axis=0))
+    zero = jnp.zeros((half, 2 * width), BF16)
+    x_pad = jnp.concatenate([zero, x2], axis=0)
+    g_pad = jnp.concatenate([g2, zero], axis=0)
+    x_col = jnp.concatenate([x_pad[half - GROUP * d : 2 * half - GROUP * d] for d in range(blocks // 2)], axis=1)
+    g_col = jnp.concatenate([g_pad[GROUP * d : GROUP * d + half] for d in range(blocks // 2)], axis=1)
+    filt2 = jnp.dot(x_col, jnp.concatenate(kerns, axis=0), preferred_element_type=F32)
+    back2 = lax.dot_general(
+        g_col, jnp.concatenate(kerns, axis=1), (((1,), (1,)), ((), ())), preferred_element_type=F32
+    )
     filt2 = filt2.astype(BF16)
     back2 = back2.astype(BF16)
     for place, i in enumerate(ORDER_OUT):
@@ -118,8 +116,7 @@
         jnp.concatenate(
             [recv_ref[p, half : half + GROUP // 2].reshape(GROUP, tokens) for p in places], axis=0
         )
-        .astype(F32)
-        .T
+        .T.astype(F32)
         for half in (0, GROUP // 2)
     ]
     out_ref[...] = (post_ref[...].astype(F32) * filt).astype(BF16)

time: 33.2 us -> 33.2 us (level)
  no operation moved by 1% of the time
where the time goes in v5:
time: 33.2 us; the launch traced here: 32.9 us
  blocking collectives  29.4 us (89%)
  Pallas kernels  2.74 us (8%)
  between operations  0.7 us (2%)
    all_to_all x1, blocking collectives, on_device(): lax.all_to_all(send, 'seq', 0, 0, tiled=True, axis_index_groups=[ORDER_IN])  18.4 us
    all_to_all x1, blocking collectives, on_device(): lax.all_to_all(back, 'seq', 0, 0, tiled=True, axis_index_groups=[ORDER_OUT])  11 us
    pallas_call x1, Pallas kernels, on_device(): pl.pallas_call(pack_kernel, out_shape=jax.ShapeDtypeStruct((n_filters, 2...  1.06 us
    pallas_call x1, Pallas kernels, on_device(): pl.pallas_call(conv_kernel, out_shape=jax.ShapeDtypeStruct((n_filters, BA...  0.89 us
    pallas_call x1, Pallas kernels, on_device(): pl.pallas_call(functools.partial(gate_kernel, length), out_shape=(grid_ou...  0.8 us

profile of v5, /device:TPU:1, one launch (start us, length us, event | category | flops | bytes accessed | tf_op | source)
XLA Modules:
  0.0 32.9 jit_solution(13290204532198477884)
XLA Ops:
  0.6 1.1 %pack.1 = bf16[16,32,128]{2,1,0:T(8,128)(2,1)S(1)} custom-call(bf16[128,256]{1,0:T(8,128)(2,1)} %post_ref.1, bf16[128,256]{1,0:T(8,128)(2,1)} %pre_ref.1, bf16[128,256]{1,0:T(8,128)(2,1)} %values_ref.1, bf16[128,256]{1,0:T(8,128)(2,1)} %gout_ref.1), custom_call_target="tpu_custom_call" | custom-call | tf_op jit(solution)/shard_map/pack/pallas_call | solution.py:139
  1.7 0.0 copy-start.4
  1.7 18.4 %all_to_all.10.recv_ref = bf16[16,32,128]{2,1,0:T(8,128)(2,1)S(1)} all-to-all(bf16[16,32,128]{2,1,0:T(8,128)(2,1)S(1)} %pack.1), channel_id=1, replica_groups={{416,448,288,224,160,96,32,480,384,320,256,192,128,64,0,352},{417,449,2..., dimensions={0} | all-to-all | bytes 262144 | tf_op jit(solution)/shard_map/all_to_all | solution.py:151
  20.1 0.0 copy-done.4
  20.1 0.9 %conv.1 = bf16[16,17,2,128]{3,2,1,0:T(2,128)(2,1)S(1)} custom-call(bf16[16,32,128]{2,1,0:T(8,128)(2,1)S(1)} %all_to_all.10.recv_ref, bf16[16,2048]{1,0:T(8,128)(2,1)S(1)} %copy-done.4), custom_call_target="tpu_custom_call" | custom-call | tf_op jit(solution)/shard_map/conv/pallas_call | solution.py:154
  21.0 0.0 copy-start
  21.0 0.0 copy-start.1
  21.0 0.0 copy-start.2
  21.1 0.0 copy-start.3
  21.1 11.0 %all_to_all.11.recv_ref = bf16[16,17,2,128]{3,2,1,0:T(2,128)(2,1)S(1)} all-to-all(bf16[16,17,2,128]{3,2,1,0:T(2,128)(2,1)S(1)} %conv.1), channel_id=1, replica_groups={{416,480,0,64,128,192,256,320,384,448,32,96,160,224,288,352},{417,481,1..., dimensions={0} | all-to-all | bytes 278528 | tf_op jit(solution)/shard_map/all_to_all | solution.py:162
  32.1 0.0 copy-done
  32.1 0.0 copy-done.1
  32.1 0.0 copy-done.2
  32.1 0.0 copy-done.3
  32.1 0.8 %gate.1 = (bf16[128,256]{1,0:T(8,128)(2,1)}, bf16[128,256]{1,0:T(8,128)(2,1)}, bf16[128,256]{1,0:T(8,128)(2,1)}, bf16[128,256]{1,0:T(8,128)(2,1)}, f32[16,128]{1,0:T(8,128)}) custom-call(bf16[16,17,2,128]{3,2,1,0:T(2,128)(2,1)S(1)} %all_to_all.11.recv_ref, bf16[128,256]{1,0:T(8,128)(2,1)S(1)} %copy-done, bf16[128,256]{1,0:T(8,128)(2,1)S(1)} %copy-done.1, ...), custom_call_target="tpu_custom_call" | custom-call | tf_op jit(solution)/shard_map/gate/pallas_call | solution.py:166
Async XLA Ops:
  1.7 18.4 %copy-start.4 = (bf16[16,2048]{1,0:T(8,128)(2,1)S(1)}, bf16[16,2048]{1,0:T(8,128)(2,1)}, u32[]{:S(2)}) copy-start(bf16[16,2048]{1,0:T(8,128)(2,1)} %filters_ref.1) | copy-start | bytes 196612
  21.0 11.0 %copy-start = (bf16[128,256]{1,0:T(8,128)(2,1)S(1)}, bf16[128,256]{1,0:T(8,128)(2,1)}, u32[]{:S(2)}) copy-start(bf16[128,256]{1,0:T(8,128)(2,1)} %post_ref.1) | copy-start | bytes 196612
  21.0 11.0 %copy-start.1 = (bf16[128,256]{1,0:T(8,128)(2,1)S(1)}, bf16[128,256]{1,0:T(8,128)(2,1)}, u32[]{:S(2)}) copy-start(bf16[128,256]{1,0:T(8,128)(2,1)} %pre_ref.1) | copy-start | bytes 196612
  21.0 11.0 %copy-start.2 = (bf16[128,256]{1,0:T(8,128)(2,1)S(1)}, bf16[128,256]{1,0:T(8,128)(2,1)}, u32[]{:S(2)}) copy-start(bf16[128,256]{1,0:T(8,128)(2,1)} %values_ref.1) | copy-start | bytes 196612
  21.1 11.0 %copy-start.3 = (bf16[128,256]{1,0:T(8,128)(2,1)S(1)}, bf16[128,256]{1,0:T(8,128)(2,1)}, u32[]{:S(2)}) copy-start(bf16[128,256]{1,0:T(8,128)(2,1)} %gout_ref.1) | copy-start | bytes 196612

commit v6 on v5

--- a/solution.py
+++ b/solution.py
@@ -47,8 +47,9 @@
     which = lax.broadcasted_iota(jnp.int32, taps.shape, 0)
     row = jnp.sum(jnp.where(which == own, taps, 0.0), axis=0, keepdims=True)
     padded = jnp.concatenate([jnp.zeros((1, width), F32), row], axis=1)
-    toep = pltpu.roll(
-        jnp.broadcast_to(padded, (width, length + width)), 0, 1, stride=1, stride_axis=0
+    eight = pltpu.roll(jnp.broadcast_to(padded, (8, length + width)), 0, 1, stride=1, stride_axis=0)
+    toep = jnp.concatenate(
+        [eight] + [pltpu.roll(eight, 8 * q, 1) for q in range(1, width // 8)], axis=0
     ).astype(BF16)
 
     at = lax.broadcasted_iota(jnp.int32, (width, width), 0)
@@ -77,36 +78,34 @@
     for place, i in enumerate(ORDER_OUT):
         back_ref[place, GROUP] = terms[:, width * i : width * (i + 1)]
 
-    def wide(v):
-        v = v.reshape(blocks // 2, 2, GROUP, width)
-        return jnp.concatenate([v[:, 0].reshape(half, width), v[:, 1].reshape(half, width)], axis=1)
-
-    half = rows // 2
-    x2 = wide(xt)
-    g2 = wide(gt)
-    kerns = []
-    for d in range(blocks // 2):
-        top = toep[:, width * (2 * d + 1) : width * (2 * d + 3)]
+    filt = None
+    back = None
+    for d in range(0, blocks, 2):
+        kern = toep[:, width * (d + 1) : width * (d + 3)]
+        keep = rows - GROUP * d
+        part = jnp.dot(xt[:keep], kern, preferred_element_type=F32)
+        near = part[:, :width]
+        far = part[: keep - GROUP, width:]
+        grads = jnp.concatenate(
+            [gt_pad[GROUP * d : rows], gt_pad[GROUP * (d + 1) : rows + GROUP]], axis=1
+        )
+        rev = lax.dot_general(
+            grads, kern, (((1,), (1,)), ((), ())), preferred_element_type=F32
+        )
         if d == 0:
-            low = jnp.concatenate([jnp.zeros((width, width), BF16), toep[:, width : 2 * width]], axis=1)
+            filt = near + jnp.concatenate([jnp.zeros((GROUP, width), F32), far], axis=0)
+            back = rev
         else:
-            low = toep[:, width * 2 * d : width * (2 * d + 2)]
-        kerns.append(jnp.concatenate([top, low], axis=0))
-    zero = jnp.zeros((half, 2 * width), BF16)
-    x_pad = jnp.concatenate([zero, x2], axis=0)
-    g_pad = jnp.concatenate([g2, zero], axis=0)
-    x_col = jnp.concatenate([x_pad[half - GROUP * d : 2 * half - GROUP * d] for d in range(blocks // 2)], axis=1)
-    g_col = jnp.concatenate([g_pad[GROUP * d : GROUP * d + half] for d in range(blocks // 2)], axis=1)
-    filt2 = jnp.dot(x_col, jnp.concatenate(kerns, axis=0), preferred_element_type=F32)
-    back2 = lax.dot_general(
-        g_col, jnp.concatenate(kerns, axis=1), (((1,), (1,)), ((), ())), preferred_element_type=F32
-    )
-    filt2 = filt2.astype(BF16)
-    back2 = back2.astype(BF16)
+            zeros = jnp.zeros((GROUP * d, width), F32)
+            more = jnp.zeros((GROUP * (d + 1), width), F32)
+            filt = filt + jnp.concatenate([zeros, near], axis=0) + jnp.concatenate([more, far], axis=0)
+            back = back + jnp.concatenate([rev, zeros], axis=0)
+    filt = filt.astype(BF16)
+    back = back.astype(BF16)
     for place, i in enumerate(ORDER_OUT):
-        at = (slice(GROUP * (i // 2), GROUP * (i // 2 + 1)), slice(width * (i % 2), width * (i % 2 + 1)))
-        back_ref[place, 0 : GROUP // 2] = filt2[at].reshape(GROUP // 2, 2, width)
-        back_ref[place, GROUP // 2 : GROUP] = back2[at].reshape(GROUP // 2, 2, width)
+        at = slice(GROUP * i, GROUP * (i + 1))
+        back_ref[place, 0 : GROUP // 2] = filt[at].reshape(GROUP // 2, 2, width)
+        back_ref[place, GROUP // 2 : GROUP] = back[at].reshape(GROUP // 2, 2, width)
 
 
 def gate_kernel(length, recv_ref, post_ref, pre_ref, values_ref, gout_ref, out_ref, gpost_ref, gpre_ref, gval_ref, gfilt_ref):

time: 33.2 us -> 33.1 us (level)
  no operation moved by 1% of the time
where the time goes in v6:
time: 33.1 us; the launch traced here: 32.8 us
  blocking collectives  29.4 us (89%)
  Pallas kernels  2.64 us (8%)
  between operations  0.7 us (2%)
    all_to_all x1, blocking collectives, on_device(): lax.all_to_all(send, 'seq', 0, 0, tiled=True, axis_index_groups=[ORDER_IN])  18.4 us
    all_to_all x1, blocking collectives, on_device(): lax.all_to_all(back, 'seq', 0, 0, tiled=True, axis_index_groups=[ORDER_OUT])  11 us
    pallas_call x1, Pallas kernels, on_device(): pl.pallas_call(pack_kernel, out_shape=jax.ShapeDtypeStruct((n_filters, 2...  1.06 us
    pallas_call x1, Pallas kernels, on_device(): pl.pallas_call(functools.partial(gate_kernel, length), out_shape=(grid_ou...  0.8 us
    pallas_call x1, Pallas kernels, on_device(): pl.pallas_call(conv_kernel, out_shape=jax.ShapeDtypeStruct((n_filters, BA...  0.78 us

profile of v6, /device:TPU:1, one launch (start us, length us, event | category | flops | bytes accessed | tf_op | source)
XLA Modules:
  0.0 32.8 jit_solution(12143737472050988035)
XLA Ops:
  0.6 1.1 %pack.1 = bf16[16,32,128]{2,1,0:T(8,128)(2,1)S(1)} custom-call(bf16[128,256]{1,0:T(8,128)(2,1)} %post_ref.1, bf16[128,256]{1,0:T(8,128)(2,1)} %pre_ref.1, bf16[128,256]{1,0:T(8,128)(2,1)} %values_ref.1, bf16[128,256]{1,0:T(8,128)(2,1)} %gout_ref.1), custom_call_target="tpu_custom_call" | custom-call | tf_op jit(solution)/shard_map/pack/pallas_call | solution.py:138
  1.7 0.0 copy-start.4
  1.7 18.4 %all_to_all.10.recv_ref = bf16[16,32,128]{2,1,0:T(8,128)(2,1)S(1)} all-to-all(bf16[16,32,128]{2,1,0:T(8,128)(2,1)S(1)} %pack.1), channel_id=1, replica_groups={{416,448,288,224,160,96,32,480,384,320,256,192,128,64,0,352},{417,449,2..., dimensions={0} | all-to-all | bytes 262144 | tf_op jit(solution)/shard_map/all_to_all | solution.py:150
  20.1 0.0 copy-done.4
  20.1 0.8 %conv.1 = bf16[16,17,2,128]{3,2,1,0:T(2,128)(2,1)S(1)} custom-call(bf16[16,32,128]{2,1,0:T(8,128)(2,1)S(1)} %all_to_all.10.recv_ref, bf16[16,2048]{1,0:T(8,128)(2,1)S(1)} %copy-done.4), custom_call_target="tpu_custom_call" | custom-call | tf_op jit(solution)/shard_map/conv/pallas_call | solution.py:153
  20.9 0.0 copy-start
  20.9 0.0 copy-start.1
  20.9 0.0 copy-start.2
  21.0 0.0 copy-start.3
  21.0 11.0 %all_to_all.11.recv_ref = bf16[16,17,2,128]{3,2,1,0:T(2,128)(2,1)S(1)} all-to-all(bf16[16,17,2,128]{3,2,1,0:T(2,128)(2,1)S(1)} %conv.1), channel_id=1, replica_groups={{416,480,0,64,128,192,256,320,384,448,32,96,160,224,288,352},{417,481,1..., dimensions={0} | all-to-all | bytes 278528 | tf_op jit(solution)/shard_map/all_to_all | solution.py:161
  32.0 0.0 copy-done
  32.0 0.0 copy-done.1
  32.0 0.0 copy-done.2
  32.0 0.0 copy-done.3
  32.0 0.8 %gate.1 = (bf16[128,256]{1,0:T(8,128)(2,1)}, bf16[128,256]{1,0:T(8,128)(2,1)}, bf16[128,256]{1,0:T(8,128)(2,1)}, bf16[128,256]{1,0:T(8,128)(2,1)}, f32[16,128]{1,0:T(8,128)}) custom-call(bf16[16,17,2,128]{3,2,1,0:T(2,128)(2,1)S(1)} %all_to_all.11.recv_ref, bf16[128,256]{1,0:T(8,128)(2,1)S(1)} %copy-done, bf16[128,256]{1,0:T(8,128)(2,1)S(1)} %copy-done.1, ...), custom_call_target="tpu_custom_call" | custom-call | tf_op jit(solution)/shard_map/gate/pallas_call | solution.py:165
Async XLA Ops:
  1.7 18.4 %copy-start.4 = (bf16[16,2048]{1,0:T(8,128)(2,1)S(1)}, bf16[16,2048]{1,0:T(8,128)(2,1)}, u32[]{:S(2)}) copy-start(bf16[16,2048]{1,0:T(8,128)(2,1)} %filters_ref.1) | copy-start | bytes 196612
  20.9 11.0 %copy-start = (bf16[128,256]{1,0:T(8,128)(2,1)S(1)}, bf16[128,256]{1,0:T(8,128)(2,1)}, u32[]{:S(2)}) copy-start(bf16[128,256]{1,0:T(8,128)(2,1)} %post_ref.1) | copy-start | bytes 196612
  20.9 11.0 %copy-start.1 = (bf16[128,256]{1,0:T(8,128)(2,1)S(1)}, bf16[128,256]{1,0:T(8,128)(2,1)}, u32[]{:S(2)}) copy-start(bf16[128,256]{1,0:T(8,128)(2,1)} %pre_ref.1) | copy-start | bytes 196612
  20.9 11.0 %copy-start.2 = (bf16[128,256]{1,0:T(8,128)(2,1)S(1)}, bf16[128,256]{1,0:T(8,128)(2,1)}, u32[]{:S(2)}) copy-start(bf16[128,256]{1,0:T(8,128)(2,1)} %values_ref.1) | copy-start | bytes 196612
  21.0 11.0 %copy-start.3 = (bf16[128,256]{1,0:T(8,128)(2,1)S(1)}, bf16[128,256]{1,0:T(8,128)(2,1)}, u32[]{:S(2)}) copy-start(bf16[128,256]{1,0:T(8,128)(2,1)} %gout_ref.1) | copy-start | bytes 196612

commit v7 on v6

--- a/solution.py
+++ b/solution.py
@@ -15,7 +15,7 @@
 VMEM = 8 * 1024 * 1024
 
 
-ORDER_IN = [13, 14, 9, 7, 5, 3, 1, 15, 12, 10, 8, 6, 4, 2, 0, 11]
+ORDER_IN = [13, 14, 9, 7, 5, 3, 0, 15, 12, 10, 8, 6, 4, 2, 1, 11]
 ORDER_OUT = [13, 15, 0, 2, 4, 6, 8, 10, 12, 14, 1, 3, 5, 7, 9, 11]
 
 

time: 33.1 us -> 33.1 us (level)
  no operation moved by 1% of the time
where the time goes in v7:
time: 33.1 us; the launch traced here: 32.8 us
  blocking collectives  29.4 us (89%)
  Pallas kernels  2.64 us (8%)
  between operations  0.7 us (2%)
    all_to_all x1, blocking collectives, on_device(): lax.all_to_all(send, 'seq', 0, 0, tiled=True, axis_index_groups=[ORDER_IN])  18.7 us
    all_to_all x1, blocking collectives, on_device(): lax.all_to_all(back, 'seq', 0, 0, tiled=True, axis_index_groups=[ORDER_OUT])  10.7 us
    pallas_call x1, Pallas kernels, on_device(): pl.pallas_call(pack_kernel, out_shape=jax.ShapeDtypeStruct((n_filters, 2...  1.06 us
    pallas_call x1, Pallas kernels, on_device(): pl.pallas_call(functools.partial(gate_kernel, length), out_shape=(grid_ou...  0.8 us
    pallas_call x1, Pallas kernels, on_device(): pl.pallas_call(conv_kernel, out_shape=jax.ShapeDtypeStruct((n_filters, BA...  0.78 us

profile of v7, /device:TPU:1, one launch (start us, length us, event | category | flops | bytes accessed | tf_op | source)
XLA Modules:
  0.0 32.8 jit_solution(16808837813265378124)
XLA Ops:
  0.6 1.1 %pack.1 = bf16[16,32,128]{2,1,0:T(8,128)(2,1)S(1)} custom-call(bf16[128,256]{1,0:T(8,128)(2,1)} %post_ref.1, bf16[128,256]{1,0:T(8,128)(2,1)} %pre_ref.1, bf16[128,256]{1,0:T(8,128)(2,1)} %values_ref.1, bf16[128,256]{1,0:T(8,128)(2,1)} %gout_ref.1), custom_call_target="tpu_custom_call" | custom-call | tf_op jit(solution)/shard_map/pack/pallas_call | solution.py:138
  1.7 0.0 copy-start.4
  1.7 18.7 %all_to_all.10.recv_ref = bf16[16,32,128]{2,1,0:T(8,128)(2,1)S(1)} all-to-all(bf16[16,32,128]{2,1,0:T(8,128)(2,1)S(1)} %pack.1), channel_id=1, replica_groups={{416,448,288,224,160,96,0,480,384,320,256,192,128,64,32,352},{417,449,2..., dimensions={0} | all-to-all | bytes 262144 | tf_op jit(solution)/shard_map/all_to_all | solution.py:150
  20.4 0.0 copy-done.4
  20.4 0.8 %conv.1 = bf16[16,17,2,128]{3,2,1,0:T(2,128)(2,1)S(1)} custom-call(bf16[16,32,128]{2,1,0:T(8,128)(2,1)S(1)} %all_to_all.10.recv_ref, bf16[16,2048]{1,0:T(8,128)(2,1)S(1)} %copy-done.4), custom_call_target="tpu_custom_call" | custom-call | tf_op jit(solution)/shard_map/conv/pallas_call | solution.py:153
  21.2 0.0 copy-start
  21.2 0.0 copy-start.1
  21.2 0.0 copy-start.2
  21.2 0.0 copy-start.3
  21.3 10.7 %all_to_all.11.recv_ref = bf16[16,17,2,128]{3,2,1,0:T(2,128)(2,1)S(1)} all-to-all(bf16[16,17,2,128]{3,2,1,0:T(2,128)(2,1)S(1)} %conv.1), channel_id=1, replica_groups={{416,480,0,64,128,192,256,320,384,448,32,96,160,224,288,352},{417,481,1..., dimensions={0} | all-to-all | bytes 278528 | tf_op jit(solution)/shard_map/all_to_all | solution.py:161
  32.0 0.0 copy-done
  32.0 0.0 copy-done.1
  32.0 0.0 copy-done.2
  32.0 0.0 copy-done.3
  32.0 0.8 %gate.1 = (bf16[128,256]{1,0:T(8,128)(2,1)}, bf16[128,256]{1,0:T(8,128)(2,1)}, bf16[128,256]{1,0:T(8,128)(2,1)}, bf16[128,256]{1,0:T(8,128)(2,1)}, f32[16,128]{1,0:T(8,128)}) custom-call(bf16[16,17,2,128]{3,2,1,0:T(2,128)(2,1)S(1)} %all_to_all.11.recv_ref, bf16[128,256]{1,0:T(8,128)(2,1)S(1)} %copy-done, bf16[128,256]{1,0:T(8,128)(2,1)S(1)} %copy-done.1, ...), custom_call_target="tpu_custom_call" | custom-call | tf_op jit(solution)/shard_map/gate/pallas_call | solution.py:165
Async XLA Ops:
  1.7 18.7 %copy-start.4 = (bf16[16,2048]{1,0:T(8,128)(2,1)S(1)}, bf16[16,2048]{1,0:T(8,128)(2,1)}, u32[]{:S(2)}) copy-start(bf16[16,2048]{1,0:T(8,128)(2,1)} %filters_ref.1) | copy-start | bytes 196612
  21.2 10.7 %copy-start = (bf16[128,256]{1,0:T(8,128)(2,1)S(1)}, bf16[128,256]{1,0:T(8,128)(2,1)}, u32[]{:S(2)}) copy-start(bf16[128,256]{1,0:T(8,128)(2,1)} %post_ref.1) | copy-start | bytes 196612
  21.2 10.7 %copy-start.1 = (bf16[128,256]{1,0:T(8,128)(2,1)S(1)}, bf16[128,256]{1,0:T(8,128)(2,1)}, u32[]{:S(2)}) copy-start(bf16[128,256]{1,0:T(8,128)(2,1)} %pre_ref.1) | copy-start | bytes 196612
  21.2 10.7 %copy-start.2 = (bf16[128,256]{1,0:T(8,128)(2,1)S(1)}, bf16[128,256]{1,0:T(8,128)(2,1)}, u32[]{:S(2)}) copy-start(bf16[128,256]{1,0:T(8,128)(2,1)} %values_ref.1) | copy-start | bytes 196612
  21.2 10.7 %copy-start.3 = (bf16[128,256]{1,0:T(8,128)(2,1)S(1)}, bf16[128,256]{1,0:T(8,128)(2,1)}, u32[]{:S(2)}) copy-start(bf16[128,256]{1,0:T(8,128)(2,1)} %gout_ref.1) | copy-start | bytes 196612
